TPU v7x, 32 devices: a whole 2x2x4 slice. The times are simulated.
32 devices in a mesh: band: 4 (over z), row: 8 (over y, x, core).
Axes of the slice: x: 2, y: 2, z: 4, core: 2. Of those that a mesh axis runs over, the one named last changes fastest.
Arguments:
- recorded: bfloat16 [1024, 1024, 512], P(('row', 'band')), may hold values from -5 to 5
- acquired: int32 [128, 128], replicated, may hold values 0 or 1
- partner: int32 [128], replicated, may hold values from 0 to 127, each once
- band_counts: int32 [4], replicated, may hold values from 1 to 12, 32 in all
- wavelet: float32 [2, 4], replicated, may hold values from -0.75 to 0.75, as said below
Outputs:
- primaries: bfloat16 [1024, 1024, 512], P(('row', 'band'))
Inputs may be any that keep to these rules, and one draw needn't show every extreme that they name: `partner`: a permutation of the 128 block indices. `band_counts`: the counts sum to 32; the largest is exactly 12. `wavelet`: each column, read as a complex number, has magnitude between 0.55 and 0.75.
All inputs are finite; a program needn't handle non-finite values.
Results may differ from a plain program's by a relative error of at most 0.0085.
Values may be sent and summed in bfloat16 or wider, within the bound.
A program may use at most 256 MiB of HBM per device.

v0:
```python
import math

import jax
import jax.numpy as jnp
from jax import lax
from jax.sharding import PartitionSpec as P

NS = 1024
NT = 512
NF = 32
FLO = 4
BS = 8
ITERS = 5


def dft_tables():
    sample_index = jnp.arange(NT, dtype=jnp.int32)
    bin_index = FLO + jnp.arange(NF, dtype=jnp.int32)
    angles = (bin_index[:, None] * sample_index[None, :] % NT).astype(jnp.float32) * (
        2.0 * math.pi / NT
    )
    cycles = jnp.concatenate([jnp.cos(angles), -jnp.sin(angles)], axis=0)
    forward = (cycles * (1.0 / math.sqrt(NT))).astype(jnp.bfloat16)
    inverse = (cycles * math.sqrt(2.0 / NF)).astype(jnp.bfloat16)
    return (forward, inverse)


def shards(recorded, acquired, partner, band_counts, wavelet):
    band_size = lax.axis_size("band")
    row_size = lax.axis_size("row")
    band_index = lax.axis_index("band")
    row_index = lax.axis_index("row")
    shot_count = recorded.shape[0]
    stations = recorded.shape[1]
    devices = band_size * row_size
    first_shot = (row_index * band_size + band_index) * shot_count
    forward, inverse = dft_tables()
    offsets = jnp.arange(BS, dtype=jnp.int32)
    mirror_index = (BS * partner[:, None] + offsets[None, :]).reshape(stations)
    present = jnp.repeat(jnp.repeat(acquired, BS, axis=0), BS, axis=1) == 1
    own_present = lax.dynamic_slice_in_dim(present, first_shot, shot_count, 0)
    linear = jnp.arange(devices, dtype=jnp.int32)
    dest_block = linear % row_size * band_size + linear // row_size
    dest_shots = (
        dest_block[:, None] * shot_count + jnp.arange(shot_count, dtype=jnp.int32)[None, :]
    ).reshape(stations)
    send_order = jnp.take(mirror_index, dest_shots)
    source_device = mirror_index // shot_count
    source_place = (
        source_device % band_size * row_size + source_device // band_size
    ) * shot_count + mirror_index % shot_count
    spectra = jnp.einsum(
        "ct,srt->csr", forward, recorded, preferred_element_type=jnp.float32
    ).astype(jnp.bfloat16)
    outgoing = jnp.take(spectra, send_order, axis=2)
    incoming = lax.all_to_all(outgoing, ("band", "row"), split_axis=2, concat_axis=2, tiled=True)
    arranged = jnp.transpose(
        incoming.reshape(2 * NF, shot_count, devices, shot_count), (0, 3, 2, 1)
    )
    arranged = arranged.reshape(2 * NF, shot_count, stations)
    mirrored = jnp.take(arranged, source_place, axis=2)
    spectra = jnp.where(own_present[None], spectra, mirrored)
    spectra = spectra.reshape(2, NF, shot_count, stations)
    band_ends = jnp.cumsum(band_counts)
    band_starts = band_ends - band_counts
    group_ids = jnp.arange(band_size, dtype=jnp.int32)
    slot_count = 3 * NF // (2 * band_size)
    slot_index = jnp.arange(slot_count, dtype=jnp.int32)
    chosen = jnp.minimum(band_starts[:, None] + slot_index[None, :], NF - 1).reshape(
        band_size * slot_count
    )
    outgoing = jnp.take(spectra, chosen, axis=1)
    local_rows = lax.all_to_all(outgoing, "band", split_axis=1, concat_axis=2, tiled=True)
    my_bins = lax.dynamic_slice_in_dim(chosen, band_index * slot_count, slot_count)
    my_group = jnp.sum((band_ends[None, :] <= my_bins[:, None]).astype(jnp.int32), axis=1)
    selector = (my_group[:, None] == group_ids[None, :]).astype(jnp.float32)
    rescale = 1.0 / math.sqrt(NS)
    wave_re = (jnp.sum(selector * wavelet[0][None, :], axis=1) * rescale)[:, None, None]
    wave_im = (jnp.sum(selector * wavelet[1][None, :], axis=1) * rescale)[:, None, None]
    whole_factor = lax.all_gather(local_rows, "row", axis=2, tiled=True)
    factor_re = (wave_re * whole_factor[0] - wave_im * whole_factor[1]).astype(jnp.bfloat16)
    factor_im = (wave_re * whole_factor[1] + wave_im * whole_factor[0]).astype(jnp.bfloat16)
    base_re = local_rows[0].astype(jnp.float32)
    base_im = local_rows[1].astype(jnp.float32)
    left_re = local_rows[0]
    left_im = local_rows[1]
    for sweep_turn in range(ITERS):
        real_part = jnp.einsum(
            "kra,kab->krb", left_re, factor_re, preferred_element_type=jnp.float32
        ) - jnp.einsum("kra,kab->krb", left_im, factor_im, preferred_element_type=jnp.float32)
        imag_part = jnp.einsum(
            "kra,kab->krb", left_re, factor_im, preferred_element_type=jnp.float32
        ) + jnp.einsum("kra,kab->krb", left_im, factor_re, preferred_element_type=jnp.float32)
        left_re = (base_re - real_part).astype(jnp.bfloat16)
        left_im = (base_im - imag_part).astype(jnp.bfloat16)
    result = jnp.stack([left_re, left_im], axis=0)
    returned = lax.all_to_all(result, "band", split_axis=2, concat_axis=1, tiled=True)
    bin_index = jnp.arange(NF, dtype=jnp.int32)
    bin_group = jnp.sum((band_ends[None, :] <= bin_index[:, None]).astype(jnp.int32), axis=1)
    bin_start = jnp.sum(
        jnp.where(bin_group[:, None] == group_ids[None, :], band_starts[None, :], 0), axis=1
    )
    slot_place = bin_group * slot_count + bin_index - bin_start
    returned = jnp.take(returned, slot_place, axis=1)
    merged = returned.reshape(2 * NF, shot_count, stations)
    output = jnp.einsum("csr,ct->srt", merged, inverse, preferred_element_type=jnp.float32)
    return output.astype(jnp.bfloat16)


def solution(mesh):
    return jax.shard_map(
        shards,
        mesh=mesh,
        in_specs=(P(("row", "band"), None, None), P(), P(), P(), P()),
        out_specs=P(("row", "band"), None, None),
        check_vma=False,
    )
```

profile of v0, /device:TPU:1, one launch (start us, length us, event | category | flops | bytes accessed | tf_op | source)
XLA Modules:
  0.0 1223.8 jit_solution(4370130761173094415)
XLA Ops:
  13.2 18.3 %convolution_convert_fusion.1 = bf16[64,32,1024]{2,0,1:T(8,128)(2,1)} fusion(bf16[32,1024,512]{2,1,0:T(8,128)(2,1)} %param.7, f32[32,512]{1,0:T(8,128)S(1)} %get-tuple-element.17, f32[32,512]{1,0:T(8,128)S(1)} %get-tuple-element.16), kind=kOutput, calls=%fused_computation.60 | convolution fusion | flops 2149679104 | bytes 37879808 | tf_op jit(solution)/shard_map/ct,srt->csr/dot_general | solution.py:52
  44.4 13.2 %gather_fusion.3 = bf16[1024,64,32]{1,2,0:T(8,128)(2,1)} fusion(bf16[64,32,1024]{0,1,2:T(8,128)(2,1)} %copy.85, s32[1024]{0:T(1024)S(1)} %broadcast_clamp_fusion.1), kind=kCustom, calls=%fused_computation.clone | custom fusion | bytes 8392704 | tf_op jit(solution)/shard_map/jit(_take)/gather | solution.py:55
  66.3 13.9 %reshape.279 = bf16[32,2,32768]{2,1,0:T(2,128)(2,1)} reshape(bf16[1024,32,64]{2,1,0:T(8,128)(2,1)} %fusion.86) | data formatting | bytes 8388608
  89.5 91.3 %all-to-all-done = bf16[32,2,32768]{2,1,0:T(2,128)(2,1)} async-done(((bf16[32,2,32768]{2,1,0:T(2,128)(2,1)}), bf16[32,2,32768]{2,1,0:T(2,128)(2,1)}, u32[]{:S(2)}, u32[]{:S(2)}) %all-to-all-start) | async-done | bytes 4194336 | tf_op jit(solution)/shard_map/all_to_all | solution.py:56
  180.7 13.8 %reshape.280 = bf16[1024,32,64]{2,1,0:T(8,128)(2,1)} reshape(bf16[32,2,32768]{2,1,0:T(2,128)(2,1)} %all-to-all-done) | data formatting | bytes 8388608
  247.1 20.0 %gather_fusion.1 = bf16[48,2,32,1024]{3,2,1,0:T(8,128)(2,1)} fusion(bf16[2,32,32,1024]{3,2,1,0:T(8,128)(2,1)} %copy.90, s32[1024]{0:T(1024)S(1)} %pad_clamp_fusion.1), kind=kCustom, calls=%fused_computation.3 | custom fusion | bytes 12583104 | tf_op jit(solution)/shard_map/jit(_take)/gather | solution.py:72
  270.5 140.9 %all_to_all.41 = bf16[2,48,32,1024]{3,2,0,1:T(8,128)(2,1)S(1)} all-to-all(bf16[2,48,32,1024]{3,2,0,1:T(8,128)(2,1)S(1)} %select_bitcast_fusion.1), channel_id=1, replica_groups=mesh['band'=4,'row'=8] {'band'}, dimensions={1} | all-to-all | bytes 12582912 | tf_op jit(solution)/shard_map/all_to_all | solution.py:73
  423.9 224.4 %all-gather.2.cloned.1.call-done = bf16[2,12,1024,1024]{3,2,1,0:T(8,128)(2,1)} async-done(((bf16[2,12,128,1024]{3,2,1,0:T(8,128)(2,1)}), bf16[2,12,1024,1024]{3,2,1,0:T(8,128)(2,1)}) %all-gather.2.cloned.1.call-update) | async-done | bytes 50331664 | tf_op jit(solution)/shard_map/all_gather | solution.py:80
  648.3 33.6 %fusion.1 = (bf16[12,1024,1024]{2,1,0:T(8,128)(2,1)}, bf16[12,1024,1024]{2,1,0:T(8,128)(2,1)}) fusion(f32[12]{0:T(128)S(1)} %get-tuple-element.18, f32[12]{0:T(128)S(1)} %get-tuple-element.19, bf16[2,12,1024,1024]{3,2,1,0:T(8,128)(2,1)} %all-gather.2.cloned.1.call-done), kind=kLoop, calls=%fused_computation.10 | loop fusion | flops 125829120 | bytes 100663392 | tf_op jit(solution)/shard_map/convert_element_type | solution.py:81
  681.9 14.3 %fusion.90 = f32[12,128,1024]{2,1,0:T(8,128)} fusion(bf16[12,128,1024]{2,1,0:T(8,128)(2,1)S(1)} %bitcast.103, bf16[12,1024,1024]{2,1,0:T(8,128)(2,1)} %get-tuple-element.10), kind=kOutput, calls=%fused_computation.161 | convolution fusion | flops 3221225472 | bytes 34603008 | tf_op jit(solution)/shard_map/kra,kab->krb/dot_general | solution.py:93
  696.2 14.4 %fusion.88 = f32[12,128,1024]{2,1,0:T(8,128)} fusion(bf16[12,128,1024]{2,1,0:T(8,128)(2,1)S(1)} %bitcast.104, bf16[12,1024,1024]{2,1,0:T(8,128)(2,1)} %get-tuple-element.11), kind=kOutput, calls=%fused_computation.159 | convolution fusion | flops 3221225472 | bytes 34603008 | tf_op jit(solution)/shard_map/kra,kab->krb/dot_general | solution.py:90
  710.6 14.6 %fusion.89 = f32[12,128,1024]{2,1,0:T(8,128)} fusion(bf16[12,128,1024]{2,1,0:T(8,128)(2,1)S(1)} %bitcast.121, bf16[12,1024,1024]{2,1,0:T(8,128)(2,1)} %get-tuple-element.11), kind=kOutput, calls=%fused_computation.160 | convolution fusion | flops 3221225472 | bytes 34603008 | tf_op jit(solution)/shard_map/kra,kab->krb/dot_general | solution.py:91
  725.1 15.0 %fusion.87 = f32[12,128,1024]{2,1,0:T(8,128)} fusion(bf16[12,128,1024]{2,1,0:T(8,128)(2,1)S(1)} %bitcast.122, bf16[12,1024,1024]{2,1,0:T(8,128)(2,1)} %get-tuple-element.10), kind=kOutput, calls=%fused_computation.158 | convolution fusion | flops 3221225472 | bytes 34603008 | tf_op jit(solution)/shard_map/kra,kab->krb/dot_general | solution.py:88
  740.1 16.5 %fusion.38 = f32[12,128,1024]{2,1,0:T(8,128)} fusion(bf16[12,1024,1024]{2,1,0:T(8,128)(2,1)} %get-tuple-element.10, bf16[12,128,1024]{2,1,0:T(8,128)(2,1)S(1)} %bitcast.105, f32[12,128,1024]{2,1,0:T(8,128)} %fusion.89, f32[12,128,1024]{2,1,0:T(8,128)} %fusion.90), kind=kOutput, calls=%fused_computation.51 | convolution fusion | flops 3227516928 | bytes 47185920 | tf_op jit(solution)/shard_map/kra,kab->krb/dot_general | solution.py:93
  756.6 16.5 %fusion.40 = f32[12,128,1024]{2,1,0:T(8,128)} fusion(bf16[12,1024,1024]{2,1,0:T(8,128)(2,1)} %get-tuple-element.11, bf16[12,128,1024]{2,1,0:T(8,128)(2,1)S(1)} %bitcast.106, f32[12,128,1024]{2,1,0:T(8,128)} %fusion.89, f32[12,128,1024]{2,1,0:T(8,128)} %fusion.90), kind=kOutput, calls=%fused_computation.52 | convolution fusion | flops 3227516928 | bytes 47185920 | tf_op jit(solution)/shard_map/kra,kab->krb/dot_general | solution.py:90
  773.1 17.4 %fusion.42 = f32[12,128,1024]{2,1,0:T(8,128)} fusion(bf16[12,1024,1024]{2,1,0:T(8,128)(2,1)} %get-tuple-element.11, bf16[12,128,1024]{2,1,0:T(8,128)(2,1)} %bitcast.113, f32[12,128,1024]{2,1,0:T(8,128)} %fusion.87, f32[12,128,1024]{2,1,0:T(8,128)} %fusion.88), kind=kOutput, calls=%fused_computation.53 | convolution fusion | flops 3227516928 | bytes 47185920 | tf_op jit(solution)/shard_map/kra,kab->krb/dot_general | solution.py:91
  790.6 17.4 %fusion.44 = f32[12,128,1024]{2,1,0:T(8,128)} fusion(bf16[12,1024,1024]{2,1,0:T(8,128)(2,1)} %get-tuple-element.10, bf16[12,128,1024]{2,1,0:T(8,128)(2,1)} %bitcast.114, f32[12,128,1024]{2,1,0:T(8,128)} %fusion.87, f32[12,128,1024]{2,1,0:T(8,128)} %fusion.88), kind=kOutput, calls=%fused_computation.54 | convolution fusion | flops 3227516928 | bytes 47185920 | tf_op jit(solution)/shard_map/kra,kab->krb/dot_general | solution.py:88
  808.0 16.6 %fusion.30 = f32[12,128,1024]{2,1,0:T(8,128)} fusion(bf16[12,1024,1024]{2,1,0:T(8,128)(2,1)} %get-tuple-element.10, bf16[12,128,1024]{2,1,0:T(8,128)(2,1)S(1)} %bitcast.107, f32[12,128,1024]{2,1,0:T(8,128)} %fusion.42, f32[12,128,1024]{2,1,0:T(8,128)} %fusion.38), kind=kOutput, calls=%fused_computation.47 | convolution fusion | flops 3227516928 | bytes 47185920 | tf_op jit(solution)/shard_map/kra,kab->krb/dot_general | solution.py:93
  824.6 16.7 %fusion.32 = f32[12,128,1024]{2,1,0:T(8,128)} fusion(bf16[12,1024,1024]{2,1,0:T(8,128)(2,1)} %get-tuple-element.11, bf16[12,128,1024]{2,1,0:T(8,128)(2,1)S(1)} %bitcast.108, f32[12,128,1024]{2,1,0:T(8,128)} %fusion.42, f32[12,128,1024]{2,1,0:T(8,128)} %fusion.38), kind=kOutput, calls=%fused_computation.48 | convolution fusion | flops 3227516928 | bytes 47185920 | tf_op jit(solution)/shard_map/kra,kab->krb/dot_general | solution.py:90
  841.3 17.4 %fusion.34 = f32[12,128,1024]{2,1,0:T(8,128)} fusion(bf16[12,1024,1024]{2,1,0:T(8,128)(2,1)} %get-tuple-element.11, bf16[12,128,1024]{2,1,0:T(8,128)(2,1)} %bitcast.115, f32[12,128,1024]{2,1,0:T(8,128)} %fusion.44, f32[12,128,1024]{2,1,0:T(8,128)} %fusion.40), kind=kOutput, calls=%fused_computation.49 | convolution fusion | flops 3227516928 | bytes 47185920 | tf_op jit(solution)/shard_map/kra,kab->krb/dot_general | solution.py:91
  858.7 17.5 %fusion.36 = f32[12,128,1024]{2,1,0:T(8,128)} fusion(bf16[12,1024,1024]{2,1,0:T(8,128)(2,1)} %get-tuple-element.10, bf16[12,128,1024]{2,1,0:T(8,128)(2,1)} %bitcast.116, f32[12,128,1024]{2,1,0:T(8,128)} %fusion.44, f32[12,128,1024]{2,1,0:T(8,128)} %fusion.40), kind=kOutput, calls=%fused_computation.50 | convolution fusion | flops 3227516928 | bytes 47185920 | tf_op jit(solution)/shard_map/kra,kab->krb/dot_general | solution.py:88
  876.2 16.5 %fusion.22 = f32[12,128,1024]{2,1,0:T(8,128)} fusion(bf16[12,1024,1024]{2,1,0:T(8,128)(2,1)} %get-tuple-element.10, bf16[12,128,1024]{2,1,0:T(8,128)(2,1)S(1)} %bitcast.109, f32[12,128,1024]{2,1,0:T(8,128)} %fusion.34, f32[12,128,1024]{2,1,0:T(8,128)} %fusion.30), kind=kOutput, calls=%fused_computation.43 | convolution fusion | flops 3227516928 | bytes 47185920 | tf_op jit(solution)/shard_map/kra,kab->krb/dot_general | solution.py:93
  892.7 16.5 %fusion.24 = f32[12,128,1024]{2,1,0:T(8,128)} fusion(bf16[12,1024,1024]{2,1,0:T(8,128)(2,1)} %get-tuple-element.11, bf16[12,128,1024]{2,1,0:T(8,128)(2,1)S(1)} %bitcast.110, f32[12,128,1024]{2,1,0:T(8,128)} %fusion.34, f32[12,128,1024]{2,1,0:T(8,128)} %fusion.30), kind=kOutput, calls=%fused_computation.44 | convolution fusion | flops 3227516928 | bytes 47185920 | tf_op jit(solution)/shard_map/kra,kab->krb/dot_general | solution.py:90
  909.3 17.4 %fusion.26 = f32[12,128,1024]{2,1,0:T(8,128)} fusion(bf16[12,1024,1024]{2,1,0:T(8,128)(2,1)} %get-tuple-element.11, bf16[12,128,1024]{2,1,0:T(8,128)(2,1)} %bitcast.117, f32[12,128,1024]{2,1,0:T(8,128)} %fusion.36, f32[12,128,1024]{2,1,0:T(8,128)} %fusion.32), kind=kOutput, calls=%fused_computation.45 | convolution fusion | flops 3227516928 | bytes 47185920 | tf_op jit(solution)/shard_map/kra,kab->krb/dot_general | solution.py:91
  926.7 17.7 %fusion.28 = f32[12,128,1024]{2,1,0:T(8,128)} fusion(bf16[12,1024,1024]{2,1,0:T(8,128)(2,1)} %get-tuple-element.10, bf16[12,128,1024]{2,1,0:T(8,128)(2,1)} %bitcast.118, f32[12,128,1024]{2,1,0:T(8,128)} %fusion.36, f32[12,128,1024]{2,1,0:T(8,128)} %fusion.32), kind=kOutput, calls=%fused_computation.46 | convolution fusion | flops 3227516928 | bytes 47185920 | tf_op jit(solution)/shard_map/kra,kab->krb/dot_general | solution.py:88
  944.4 16.6 %fusion.16 = f32[12,128,1024]{2,1,0:T(8,128)} fusion(bf16[12,1024,1024]{2,1,0:T(8,128)(2,1)} %get-tuple-element.11, bf16[12,128,1024]{2,1,0:T(8,128)(2,1)S(1)} %bitcast.111, f32[12,128,1024]{2,1,0:T(8,128)} %fusion.26, f32[12,128,1024]{2,1,0:T(8,128)} %fusion.22), kind=kOutput, calls=%fused_computation.40 | convolution fusion | flops 3227516928 | bytes 47185920 | tf_op jit(solution)/shard_map/kra,kab->krb/dot_general | solution.py:90
  961.0 17.4 %fusion.18 = f32[12,128,1024]{2,1,0:T(8,128)} fusion(bf16[12,1024,1024]{2,1,0:T(8,128)(2,1)} %get-tuple-element.11, bf16[12,128,1024]{2,1,0:T(8,128)(2,1)} %bitcast.119, f32[12,128,1024]{2,1,0:T(8,128)} %fusion.28, f32[12,128,1024]{2,1,0:T(8,128)} %fusion.24), kind=kOutput, calls=%fused_computation.41 | convolution fusion | flops 3227516928 | bytes 47185920 | tf_op jit(solution)/shard_map/kra,kab->krb/dot_general | solution.py:91
  978.4 21.2 %fusion.48 = bf16[1,12,128,1024]{3,2,1,0:T(8,128)(2,1)} fusion(f32[12,128,1024]{2,1,0:T(8,128)} %fusion.16, bf16[12,128,1024]{2,1,0:T(8,128)(2,1)} %bitcast.120, bf16[12,1024,1024]{2,1,0:T(8,128)(2,1)} %get-tuple-element.10, f32[12,128,1024]{2,1,0:T(8,128)} %fusion.28, f32[12,128,1024]{2,1,0:T(8,128)} %fusion.24), kind=kOutput, calls=%fused_computation.59 | convolution fusion | flops 3233808384 | bytes 50331648 | tf_op jit(solution)/shard_map/kra,kab->krb/dot_general | solution.py:88
  999.6 17.7 %fusion.47 = bf16[1,12,128,1024]{3,2,1,0:T(8,128)(2,1)} fusion(f32[12,128,1024]{2,1,0:T(8,128)} %fusion.18, bf16[12,128,1024]{2,1,0:T(8,128)(2,1)S(1)} %bitcast.112, bf16[12,1024,1024]{2,1,0:T(8,128)(2,1)} %get-tuple-element.10, f32[12,128,1024]{2,1,0:T(8,128)} %fusion.26, f32[12,128,1024]{2,1,0:T(8,128)} %fusion.22), kind=kOutput, calls=%fused_computation.58 | convolution fusion | flops 3233808384 | bytes 50331648 | tf_op jit(solution)/shard_map/kra,kab->krb/dot_general | solution.py:93
  1020.8 19.2 %copy.95 = bf16[2,12,128,1024]{3,0,1,2:T(2,128)(2,1)} copy(bf16[2,12,128,1024]{3,2,1,0:T(8,128)(2,1)S(1)} %pad_maximum_fusion) | data formatting | bytes 12582912 | tf_op jit(solution)/shard_map/stack | solution.py:96
  1045.7 137.7 %all-to-all-done.2 = bf16[2,12,128,1024]{3,0,1,2:T(2,128)(2,1)} async-done(((bf16[2,12,128,1024]{3,0,1,2:T(2,128)(2,1)}), bf16[2,12,128,1024]{3,0,1,2:T(2,128)(2,1)}, u32[]{:S(2)}, u32[]{:S(2)}) %all-to-all-start.2) | async-done | bytes 6291488 | tf_op jit(solution)/shard_map/all_to_all | solution.py:97
  1202.2 14.4 %convolution_convert_fusion = bf16[32,1024,512]{2,1,0:T(8,128)(2,1)} fusion(bf16[64,32,1024]{2,1,0:T(8,128)(2,1)S(1)} %bitcast_select_fusion, f32[32,512]{1,0:T(8,128)S(1)} %copy-done.5, f32[32,512]{1,0:T(8,128)S(1)} %copy-done.3), kind=kOutput, calls=%fused_computation.15 | convolution fusion | flops 2164359168 | bytes 37879808 | tf_op jit(solution)/shard_map/csr,ct->srt/dot_general | solution.py:106
  (92 shorter events, 133.6 us)
Async XLA Ops:
  12.6 0.6 copy-start.2
  12.6 0.6 copy-start.4
  80.2 7.2 copy-start.10
  80.2 7.9 copy-start.6
  80.2 100.5 %all-to-all-start = ((bf16[32,2,32768]{2,1,0:T(2,128)(2,1)}), bf16[32,2,32768]{2,1,0:T(2,128)(2,1)}, u32[]{:S(2)}, u32[]{:S(2)}) async-start(bf16[32,2,32768]{2,1,0:T(2,128)(2,1)} %reshape.279), calls=%async_computation | async-start | bytes 8388608 | tf_op jit(solution)/shard_map/all_to_all | solution.py:56
  87.4 561.0 %all-gather.2.cloned.1.call-start = ((), (), s32[]{:S(2)}) async-start(), calls=%async_computation.3 | async-start | bytes 56623104 | tf_op jit(solution)/shard_map/all_gather | solution.py:80
  87.6 328.5 %copy-start.11 = (s32[4,1]{0,1:T(1,128)}, s32[4,1]{0,1:T(1,128)S(1)}, u32[]{:S(2)}) copy-start(s32[4,1]{0,1:T(1,128)S(1)} %reduce-window.8) | copy-start | bytes 52
  87.6 0.5 copy-start.8
  411.4 4.6 copy-start.1
  416.0 0.7 copy-start.7
  696.2 14.4 %copy-start = (bf16[1,12,4,32,1024]{4,3,2,1,0:T(8,128)(2,1)S(1)}, bf16[1,12,4,32,1024]{4,3,2,1,0:T(8,128)(2,1)}, u32[]{:S(2)}) copy-start(bf16[1,12,4,32,1024]{4,3,2,1,0:T(8,128)(2,1)} %copy.92) | copy-start | bytes 9437188
  1040.0 5.4 copy-start.12
  1040.0 5.5 copy-start.9
  1040.0 143.4 %all-to-all-start.2 = ((bf16[2,12,128,1024]{3,0,1,2:T(2,128)(2,1)}), bf16[2,12,128,1024]{3,0,1,2:T(2,128)(2,1)}, u32[]{:S(2)}, u32[]{:S(2)}) async-start(bf16[2,12,128,1024]{3,0,1,2:T(2,128)(2,1)} %copy.95), calls=%async_computation.2 | async-start | bytes 12582912 | tf_op jit(solution)/shard_map/all_to_all | solution.py:97
  1201.3 0.8 copy-start.3
  1201.3 0.9 copy-start.5
Sparse Core Ops, SparseCore 0:
  416.2 232.1 all-gather.1
where the time goes:
time: 1230 us; the launch traced here: 1220 us
  waiting for transfers between devices  453 us (37%)
  matrix products  368 us (30%)
  local copies, waits for them, and re-layouts  179 us (15%)
  blocking collectives  141 us (11%)
  other arithmetic  55.7 us (5%)
  between operations  14.1 us (1%)
  starting transfers between devices  12.6 us (1%)
    all_gather x1, waiting for transfers between devices, shards(): whole_factor = lax.all_gather(local_rows, 'row', axis=2, tiled=True)  224 us
    all_to_all x1, blocking collectives, shards(): lax.all_to_all(outgoing, 'band', split_axis=1, concat_axis=2, tiled=True)  141 us
    all_to_all x1, waiting for transfers between devices, shards(): lax.all_to_all(result, 'band', split_axis=2, concat_axis=1, tiled=True)  138 us
    all_to_all x1, waiting for transfers between devices, shards(): lax.all_to_all(outgoing, ('band', 'row'), split_axis=2, concat_axis=2, ti...  91.3 us
    dot_general x5, matrix products, shards(): jnp.einsum('kra,kab->krb', left_re, factor_re, preferred_element_type=jnp...  88.9 us
    dot_general x5, matrix products, shards(): jnp.einsum('kra,kab->krb', left_re, factor_im, preferred_element_type=jnp...  84.3 us
    dot_general x5, matrix products, shards(): jnp.einsum('kra,kab->krb', left_im, factor_re, preferred_element_type=jnp...  81.6 us
    dot_general x5, matrix products, shards(): jnp.einsum('kra,kab->krb', left_im, factor_im, preferred_element_type=jnp...  80.7 us
  transfers between devices with their start and end apart: 3, of which 3 were waited for; matrix products, arithmetic and copies ran while one was open for 1% of the time, Pallas kernels for 0%

commit v1 on v0

v1 whole, which is shorter than its diff:
```python
import math

import jax
import jax.numpy as jnp
from jax import lax
from jax.experimental import pallas as pl
from jax.experimental.pallas import tpu as pltpu
from jax.sharding import PartitionSpec as P

NT = 512
NF = 32
FLO = 4
BS = 8
ITERS = 5
CHUNKS = 2
AXES = ("row", "band")


def dft_tables():
    sample_index = jnp.arange(NT, dtype=jnp.int32)
    bin_index = FLO + jnp.arange(NF, dtype=jnp.int32)
    angles = (bin_index[:, None] * sample_index[None, :] % NT).astype(jnp.float32) * (
        2.0 * math.pi / NT
    )
    cycles = jnp.concatenate([jnp.cos(angles), -jnp.sin(angles)], axis=0)
    forward = (cycles * (1.0 / math.sqrt(NT))).astype(jnp.bfloat16)
    inverse = (cycles * math.sqrt(2.0 / NF)).astype(jnp.bfloat16)
    return (forward, inverse)


def solve_kernel(tile, base_ref, factor_ref, out_ref, held):
    width = base_ref.shape[1]
    for turn in range(ITERS):
        left = base_ref if turn == 0 else held.at[(turn + 1) % 2]
        into = out_ref if turn == ITERS - 1 else held.at[turn % 2]

        @pl.loop(0, width // tile)
        def _(step):
            columns = pl.ds(pl.multiple_of(step * tile, tile), tile)
            product = jnp.dot(
                left[...], factor_ref[:, columns], preferred_element_type=jnp.float32
            )
            into[:, columns] = (base_ref[:, columns].astype(jnp.float32) - product).astype(
                jnp.bfloat16
            )


def solve(base, factor):
    rows, width = base.shape
    tile = min(512, width)
    vmem = pl.BlockSpec(memory_space=pltpu.VMEM)
    return pl.pallas_call(
        lambda *refs: solve_kernel(tile, *refs),
        out_shape=jax.ShapeDtypeStruct((rows, width), jnp.bfloat16),
        in_specs=[vmem, vmem],
        out_specs=vmem,
        scratch_shapes=[pltpu.VMEM((2, rows, width), jnp.bfloat16)],
        compiler_params=pltpu.CompilerParams(vmem_limit_bytes=48 << 20),
        cost_estimate=pl.CostEstimate(
            flops=2 * ITERS * rows * width * width,
            bytes_accessed=2 * (2 * rows * width + width * width),
            transcendentals=0,
        ),
        name="solve",
    )(base, factor)


def restore_kernel(data_ref, table_ref, *rest):
    out_ref = rest[-1]
    out_ref[0] = lax.dot_general(
        data_ref[0], table_ref[...], (((0,), (0,)), ((), ())), preferred_element_type=jnp.float32
    ).astype(jnp.bfloat16)


def restore(data, table, whole, first, shot_count):
    count, parts, stations = data.shape
    samples = table.shape[1]
    in_specs = [
        pl.BlockSpec((1, parts, stations), lambda i: (i, 0, 0)),
        pl.BlockSpec((parts, samples), lambda i: (0, 0)),
    ]
    args = [data, table]
    aliases = {}
    if whole is not None:
        in_specs.append(pl.BlockSpec(memory_space=pl.ANY))
        args.append(whole)
        aliases = {2: 0}
    return pl.pallas_call(
        restore_kernel,
        grid=(count,),
        out_shape=jax.ShapeDtypeStruct((shot_count, stations, samples), jnp.bfloat16),
        in_specs=in_specs,
        out_specs=pl.BlockSpec((1, stations, samples), lambda i: (first + i, 0, 0)),
        input_output_aliases=aliases,
        compiler_params=pltpu.CompilerParams(vmem_limit_bytes=32 << 20),
        cost_estimate=pl.CostEstimate(
            flops=2 * count * parts * stations * samples,
            bytes_accessed=2 * count * stations * (samples + parts),
            transcendentals=0,
        ),
        name="restore",
    )(*args)


def shards(recorded, acquired, partner, band_counts, wavelet):
    band_size = lax.axis_size("band")
    devices = band_size * lax.axis_size("row")
    shot_count, stations, _ = recorded.shape
    copies = devices // NF
    here = lax.axis_index("row") * band_size + lax.axis_index("band")
    forward, inverse = dft_tables()

    chunks = min(CHUNKS, shot_count // copies)
    size = shot_count // chunks
    pieces = []
    for chunk in range(chunks):
        part = lax.slice_in_dim(recorded, chunk * size, (chunk + 1) * size, axis=0)
        spectra = jnp.einsum(
            "ct,srt->csr", forward, part, preferred_element_type=jnp.float32
        ).astype(jnp.bfloat16)
        spectra = jnp.swapaxes(spectra.reshape(2, NF, size, stations), 0, 1)
        if copies > 1:
            spectra = jnp.repeat(spectra, copies, axis=0)
        pieces.append(lax.all_to_all(spectra, AXES, split_axis=0, concat_axis=0, tiled=True))
    data = jnp.stack(pieces, axis=2)
    data = jnp.swapaxes(data, 0, 1).reshape(2, stations, stations)

    offsets = jnp.arange(BS, dtype=jnp.int32)
    mirror_index = (BS * partner[:, None] + offsets[None, :]).reshape(stations)
    station = jnp.arange(stations, dtype=jnp.int32)
    permute = (mirror_index[:, None] == station[None, :]).astype(jnp.bfloat16)
    present = jnp.repeat(jnp.repeat(acquired, BS, axis=0), BS, axis=1) == 1
    filled = []
    for part in range(2):
        moved = jnp.dot(permute, data[part], preferred_element_type=jnp.float32)
        mirrored = lax.dot_general(
            permute,
            moved.astype(jnp.bfloat16),
            (((1,), (1,)), ((), ())),
            preferred_element_type=jnp.float32,
        ).astype(jnp.bfloat16)
        filled.append(jnp.where(present, data[part], mirrored))
    base_re, base_im = filled
    own_bin = here // copies
    own_group = jnp.sum((jnp.cumsum(band_counts) <= own_bin).astype(jnp.int32))
    chosen = (jnp.arange(band_counts.shape[0], dtype=jnp.int32) == own_group).astype(jnp.float32)
    rescale = 1.0 / math.sqrt(stations)
    wave_re = jnp.sum(chosen * wavelet[0]) * rescale
    wave_im = jnp.sum(chosen * wavelet[1]) * rescale
    wide_re = base_re.astype(jnp.float32)
    wide_im = base_im.astype(jnp.float32)
    factor_re = (wave_re * wide_re - wave_im * wide_im).astype(jnp.bfloat16)
    factor_im = (wave_re * wide_im + wave_im * wide_re).astype(jnp.bfloat16)
    factor = jnp.concatenate(
        [
            jnp.concatenate([factor_re, factor_im], axis=1),
            jnp.concatenate([-factor_im, factor_re], axis=1),
        ],
        axis=0,
    )
    base = jnp.concatenate([base_re, base_im], axis=1)

    own_count = shot_count // copies
    base = base.reshape(devices, shot_count, 2 * stations)
    if copies > 1:
        base = lax.dynamic_slice_in_dim(base, here % copies * own_count, own_count, axis=1)
    size = own_count // chunks
    output = None
    for chunk in range(chunks):
        rows = lax.slice_in_dim(base, chunk * size, (chunk + 1) * size, axis=1)
        solved = solve(rows.reshape(devices * size, 2 * stations), factor)
        solved = solved.reshape(devices, size, 2 * stations)
        back = lax.all_to_all(solved, AXES, split_axis=0, concat_axis=0, tiled=True)
        back = back.reshape(NF, copies, size, 2, stations)
        back = jnp.transpose(back, (1, 2, 3, 0, 4)).reshape(copies, size, 2 * NF, stations)
        for copy in range(copies):
            output = restore(
                back[copy], inverse, output, copy * own_count + chunk * size, shot_count
            )
    return output


def solution(mesh):
    return jax.shard_map(
        shards,
        mesh=mesh,
        in_specs=(P(AXES, None, None), P(), P(), P(), P()),
        out_specs=P(AXES, None, None),
        check_vma=False,
    )
```

time: 1230 us -> 356 us (0.29)
  matrix products: 368 us -> 39.5 us
  waiting for transfers between devices: 453 us -> 134 us
  local copies, waits for them, and re-layouts: 179 us -> 28.5 us
  blocking collectives: 141 us -> 0 us
  Pallas kernels: 0 us -> 83.9 us
    dot_general x22 -> x4, matrix products: 368 us -> 39.5 us  [the longest x2 23.1 us: shards(): jnp.einsum('ct,srt->csr', forward, part, preferred_element_type=jnp.float32)]
    all_gather x1 -> x0, waiting for transfers between devices: 224 us -> none  [shards(): whole_factor = lax.all_gather(local_rows, 'row', axis=2, tiled=True)]
    all_to_all x1 -> x0, blocking collectives: 141 us -> none  [shards(): lax.all_to_all(outgoing, 'band', split_axis=1, concat_axis=2, tiled=True)]
    all_to_all x2 -> x4, waiting for transfers between devices: 229 us -> 134 us  [the longest x2 74.5 us: shards(): lax.all_to_all(spectra, AXES, split_axis=0, concat_axis=0, tiled=True)]
    pallas_call x0 -> x4, Pallas kernels: none -> 83.9 us  [the longest x2 60 us: solve(): pl.pallas_call(lambda *refs: solve_kernel(tile, *refs), out_shape=jax.Sha...]
    gather x7 -> x0, local copies, waits for them, and re-layouts: 68.8 us -> none  [the longest x2 22.9 us: shards(): mirrored = jnp.take(arranged, source_place, axis=2)]
    concatenate x0 -> x2, other arithmetic: none -> 36.8 us  [the longest x1 36.4 us: shards(): jnp.concatenate([jnp.concatenate([factor_re, factor_im], axis=1), jnp.con...]
    convert_element_type x1, other arithmetic: 33.6 us -> 0.01 us  [dft_tables(): inverse = (cycles * math.sqrt(2.0 / NF)).astype(jnp.bfloat16)]
  transfers between devices with their start and end apart: 3 -> 4, of which waited for: 3 -> 4; matrix products, arithmetic and copies ran while one was open for 1% -> 8% of each run, Pallas kernels for 0% -> 9%
where the time goes in v1:
time: 356 us; the launch traced here: 350 us
  waiting for transfers between devices  134 us (38%)
  Pallas kernels  83.9 us (24%)
  other arithmetic  44.3 us (12%)
  matrix products  39.5 us (11%)
  local copies, waits for them, and re-layouts  28.5 us (8%)
  starting transfers between devices  17.7 us (5%)
    all_to_all x2, waiting for transfers between devices, shards(): lax.all_to_all(spectra, AXES, split_axis=0, concat_axis=0, tiled=True)  74.5 us
    pallas_call x2, Pallas kernels, solve(): pl.pallas_call(lambda *refs: solve_kernel(tile, *refs), out_shape=jax.Sha...  60 us
    all_to_all x2, waiting for transfers between devices, shards(): back = lax.all_to_all(solved, AXES, split_axis=0, concat_axis=0, tiled=True)  59.5 us
    concatenate x1, other arithmetic, shards(): jnp.concatenate([jnp.concatenate([factor_re, factor_im], axis=1), jnp.con...  36.4 us
    pallas_call x2, Pallas kernels, restore(): pl.pallas_call(restore_kernel, grid=(count,), out_shape=jax.ShapeDtypeStr...  23.9 us
    dot_general x2, matrix products, shards(): jnp.einsum('ct,srt->csr', forward, part, preferred_element_type=jnp.float32)  23.1 us
    dot_general x2, matrix products, shards(): lax.dot_general(permute, moved.astype(jnp.bfloat16), (((1,), (1,)), ((),...  16.4 us
    all_to_all x2, starting transfers between devices, shards(): lax.all_to_all(spectra, AXES, split_axis=0, concat_axis=0, tiled=True)  10.7 us
  transfers between devices with their start and end apart: 4, of which 4 were waited for; matrix products, arithmetic and copies ran while one was open for 8% of the time, Pallas kernels for 9%

profile of v1, /device:TPU:1, one launch (start us, length us, event | category | flops | bytes accessed | tf_op | source)
XLA Modules:
  0.0 349.7 jit_solution(13724987054135208532)
XLA Ops:
  0.4 10.9 %fusion.21 = bf16[64,16,1024]{2,0,1:T(8,128)(2,1)S(1)} fusion(bf16[32,1024,512]{2,1,0:T(8,128)(2,1)} %param.5, f32[32,512]{1,0:T(8,128)S(1)} %get-tuple-element.14, f32[32,512]{1,0:T(8,128)S(1)} %get-tuple-element.13), kind=kOutput, calls=%fused_computation.32 | convolution fusion | flops 1074888704 | bytes 19005440 | tf_op jit(solution)/shard_map/ct,srt->csr/dot_general | solution.py:118
  11.3 2.5 copy.44
  13.7 7.1 %all-to-all-start.1 = ((bf16[32,2,16,1024]{3,2,1,0:T(8,128)(2,1)}), bf16[32,2,16,1024]{3,2,1,0:T(8,128)(2,1)S(1)}, u32[]{:S(2)}, u32[]{:S(2)}) async-start(bf16[32,2,16,1024]{3,2,1,0:T(8,128)(2,1)} %bitcast.36), calls=%async_computation.1 | async-start | bytes 4194304 | tf_op jit(solution)/shard_map/all_to_all | solution.py:124
  20.8 12.2 %fusion.18 = bf16[64,16,1024]{2,0,1:T(8,128)(2,1)} fusion(bf16[32,1024,512]{2,1,0:T(8,128)(2,1)} %param.5, f32[32,512]{1,0:T(8,128)S(1)} %get-tuple-element.14, f32[32,512]{1,0:T(8,128)S(1)} %get-tuple-element.13), kind=kOutput, calls=%fused_computation.31 | convolution fusion | flops 1074888704 | bytes 19005440 | tf_op jit(solution)/shard_map/ct,srt->csr/dot_general | solution.py:118
  33.0 4.1 %copy.45 = bf16[2,32,16,1024]{3,2,0,1:T(8,128)(2,1)} copy(bf16[2,32,16,1024]{3,1,0,2:T(8,128)(2,1)} %bitcast.49) | data formatting | bytes 4194304 | tf_op jit(solution)/shard_map/reshape | solution.py:121
  37.2 31.9 %all-to-all-done.1 = bf16[32,2,16,1024]{3,2,1,0:T(8,128)(2,1)S(1)} async-done(((bf16[32,2,16,1024]{3,2,1,0:T(8,128)(2,1)}), bf16[32,2,16,1024]{3,2,1,0:T(8,128)(2,1)S(1)}, u32[]{:S(2)}, u32[]{:S(2)}) %all-to-all-start.1) | async-done | bytes 2097184 | tf_op jit(solution)/shard_map/all_to_all | solution.py:124
  69.1 3.6 %all-to-all-start = ((bf16[32,2,16,1024]{3,2,1,0:T(8,128)(2,1)}), bf16[32,2,16,1024]{3,2,1,0:T(8,128)(2,1)}, u32[]{:S(2)}, u32[]{:S(2)}) async-start(bf16[32,2,16,1024]{3,2,1,0:T(8,128)(2,1)} %bitcast.37), calls=%async_computation | async-start | bytes 4194304 | tf_op jit(solution)/shard_map/all_to_all | solution.py:124
  72.9 0.6 fusion.40
  73.6 1.3 fusion.38
  77.0 1.2 copy.34
  78.2 42.6 %all-to-all-done = bf16[32,2,16,1024]{3,2,1,0:T(8,128)(2,1)} async-done(((bf16[32,2,16,1024]{3,2,1,0:T(8,128)(2,1)}), bf16[32,2,16,1024]{3,2,1,0:T(8,128)(2,1)}, u32[]{:S(2)}, u32[]{:S(2)}) %all-to-all-start) | async-done | bytes 2097184 | tf_op jit(solution)/shard_map/all_to_all | solution.py:124
  120.9 2.0 maximum_bitcast_fusion
  122.8 0.8 fusion.48
  123.7 1.5 copy.32
  125.2 1.5 copy.35
  126.7 6.9 %convert_select_fusion = bf16[1024,1024]{1,0:T(8,128)(2,1)S(1)} fusion(pred[1024,1024]{1,0:T(32,128)(4,1)S(1)} %copy.34, bf16[1024,1024]{1,0:T(8,128)(2,1)} %bitcast.47, s32[1024]{0:T(1024)S(1)} %add.53), kind=kOutput, calls=%fused_computation.22 | convolution fusion | flops 4300210176 | bytes 5246976 | tf_op jit(solution)/shard_map/dot_general | solution.py:136
  133.6 9.5 %fusion.5 = (bf16[1024,1024]{1,0:T(8,128)(2,1)}, bf16[1024,1024]{1,0:T(8,128)(2,1)}) fusion(bf16[1024,1024]{1,0:T(8,128)(2,1)S(1)} %convert_select_fusion, f32[]{:T(128)S(6)} %mul.96, f32[]{:T(128)S(6)} %mul.92, pred[1024,1024]{1,0:T(32,128)(4,1)S(1)} %copy.34, bf16[1024,1024]{1,0:T(8,128)(2,1)} %bitcast.46, s32[1024]{0:T(1024)S(1)} %add.53), kind=kOutput, calls=%fused_computation.10 | convolution fusion | flops 4306501632 | bytes 9441288 | tf_op jit(solution)/shard_map/dot_general | solution.py:136
  143.1 3.0 fusion.45
  147.0 1.1 copy-done.1
  148.1 36.4 %maximum_maximum_fusion.refs_1_ = bf16[2048,2048]{1,0:T(8,128)(2,1)} fusion(bf16[1024,1024]{1,0:T(8,128)(2,1)S(1)} %copy-done.1, bf16[1024,1024]{1,0:T(8,128)(2,1)S(1)} %get-tuple-element.7, bf16[1024,1024]{1,0:T(8,128)(2,1)S(1)} %get-tuple-element.8), kind=kLoop, calls=%fused_computation.4 | loop fusion | flops 33554432 | bytes 14680064 | tf_op jit(solution)/shard_map/concatenate | solution.py:154
  184.5 30.1 %solve.3 = bf16[512,2048]{1,0:T(8,128)(2,1)} custom-call(bf16[512,2048]{1,0:T(8,128)(2,1)S(1)} %bitcast.41, bf16[2048,2048]{1,0:T(8,128)(2,1)} %maximum_maximum_fusion.refs_1_), custom_call_target="tpu_custom_call" | custom-call | flops 21474836480 | bytes 12582912 | tf_op jit(solution)/shard_map/solve/pallas_call | solution.py:52
  214.6 3.5 all-to-all-start.3
  218.1 29.9 %solve.2 = bf16[512,2048]{1,0:T(8,128)(2,1)} custom-call(bf16[512,2048]{1,0:T(8,128)(2,1)S(1)} %bitcast.40, bf16[2048,2048]{1,0:T(8,128)(2,1)} %maximum_maximum_fusion.refs_1_), custom_call_target="tpu_custom_call" | custom-call | flops 21474836480 | bytes 12582912 | tf_op jit(solution)/shard_map/solve/pallas_call | solution.py:52
  247.9 18.4 %all-to-all-done.3 = bf16[32,16,2048]{2,1,0:T(8,128)(2,1)} async-done(((bf16[32,16,2048]{2,1,0:T(8,128)(2,1)}), bf16[32,16,2048]{2,1,0:T(8,128)(2,1)}, u32[]{:S(2)}, u32[]{:S(2)}) %all-to-all-start.3) | async-done | bytes 2097184 | tf_op jit(solution)/shard_map/all_to_all | solution.py:173
  266.4 3.5 all-to-all-start.2
  269.9 4.5 %reshape.94 = bf16[32,1,16,2,1024]{4,3,2,0,1:T(2,128)(2,1)} reshape(bf16[32,16,2048]{2,1,0:T(8,128)(2,1)} %all-to-all-done.3) | data formatting | bytes 4194304 | tf_op jit(solution)/shard_map/reshape | solution.py:174
  274.3 2.7 copy.39
  277.1 41.1 %all-to-all-done.2 = bf16[32,16,2048]{2,1,0:T(8,128)(2,1)} async-done(((bf16[32,16,2048]{2,1,0:T(8,128)(2,1)}), bf16[32,16,2048]{2,1,0:T(8,128)(2,1)}, u32[]{:S(2)}, u32[]{:S(2)}) %all-to-all-start.2) | async-done | bytes 2097184 | tf_op jit(solution)/shard_map/all_to_all | solution.py:173
  318.1 4.5 %reshape.91 = bf16[32,1,16,2,1024]{4,3,2,0,1:T(2,128)(2,1)} reshape(bf16[32,16,2048]{2,1,0:T(8,128)(2,1)} %all-to-all-done.2) | data formatting | bytes 4194304 | tf_op jit(solution)/shard_map/reshape | solution.py:174
  322.6 2.7 copy.38
  325.3 12.0 %restore.2.rest_0_ = bf16[32,1024,512]{2,1,0:T(8,128)(2,1)} custom-call(bf16[16,64,1024]{2,1,0:T(8,128)(2,1)S(1)} %bitcast.38, bf16[64,512]{1,0:T(8,128)(2,1)S(1)} %multiply_convert_fusion.table_ref), custom_call_target="tpu_custom_call" | custom-call | flops 1073741824 | bytes 18874368 | tf_op jit(solution)/shard_map/restore/pallas_call | solution.py:88
  337.3 12.0 %restore.3 = bf16[32,1024,512]{2,1,0:T(8,128)(2,1)} custom-call(bf16[16,64,1024]{2,1,0:T(8,128)(2,1)S(1)} %bitcast.39, bf16[64,512]{1,0:T(8,128)(2,1)S(1)} %multiply_convert_fusion.table_ref, bf16[32,1024,512]{2,1,0:T(8,128)(2,1)} %restore.2.rest_0_), custom_call_target="tpu_custom_call", output_to_operand_aliasing={{}: (2, {})} | custom-call | flops 1073741824 | bytes 18874368 | tf_op jit(solution)/shard_map/restore/pallas_call | solution.py:88
  (24 shorter events, 2.4 us)
Async XLA Ops:
  13.7 55.4 %all-to-all-start.1 = ((bf16[32,2,16,1024]{3,2,1,0:T(8,128)(2,1)}), bf16[32,2,16,1024]{3,2,1,0:T(8,128)(2,1)S(1)}, u32[]{:S(2)}, u32[]{:S(2)}) async-start(bf16[32,2,16,1024]{3,2,1,0:T(8,128)(2,1)} %bitcast.36), calls=%async_computation.1 | async-start | bytes 4194304 | tf_op jit(solution)/shard_map/all_to_all | solution.py:124
  33.0 39.7 %copy-start.4 = (s32[4]{0:T(128)S(1)}, s32[4]{0:T(128)}, u32[]{:S(2)}) copy-start(s32[4]{0:T(128)} %param.8) | copy-start | bytes 52
  33.0 40.5 %copy-start.3 = (f32[2,4]{1,0:T(2,128)S(1)}, f32[2,4]{1,0:T(2,128)}, u32[]{:S(2)}) copy-start(f32[2,4]{1,0:T(2,128)} %param.9) | copy-start | bytes 100
  33.0 43.0 %copy-start.5 = (s32[128]{0:T(128)S(1)}, s32[128]{0:T(128)}, u32[]{:S(2)}) copy-start(s32[128]{0:T(128)} %param.7) | copy-start | bytes 1540
  33.0 43.2 %copy-start.2 = (s32[128,128]{1,0:T(8,128)S(1)}, s32[128,128]{1,0:T(8,128)}, u32[]{:S(2)}) copy-start(s32[128,128]{1,0:T(8,128)} %param.6) | copy-start | bytes 196612
  69.1 51.8 %all-to-all-start = ((bf16[32,2,16,1024]{3,2,1,0:T(8,128)(2,1)}), bf16[32,2,16,1024]{3,2,1,0:T(8,128)(2,1)}, u32[]{:S(2)}, u32[]{:S(2)}) async-start(bf16[32,2,16,1024]{3,2,1,0:T(8,128)(2,1)} %bitcast.37), calls=%async_computation | async-start | bytes 4194304 | tf_op jit(solution)/shard_map/all_to_all | solution.py:124
  143.1 3.0 copy-start
  146.5 1.6 copy-start.1
  214.6 51.8 %all-to-all-start.3 = ((bf16[32,16,2048]{2,1,0:T(8,128)(2,1)}), bf16[32,16,2048]{2,1,0:T(8,128)(2,1)}, u32[]{:S(2)}, u32[]{:S(2)}) async-start(bf16[32,16,2048]{2,1,0:T(8,128)(2,1)} %bitcast.21), calls=%async_computation.3 | async-start | bytes 4194304 | tf_op jit(solution)/shard_map/all_to_all | solution.py:173
  266.4 51.8 %all-to-all-start.2 = ((bf16[32,16,2048]{2,1,0:T(8,128)(2,1)}), bf16[32,16,2048]{2,1,0:T(8,128)(2,1)}, u32[]{:S(2)}, u32[]{:S(2)}) async-start(bf16[32,16,2048]{2,1,0:T(8,128)(2,1)} %bitcast.17), calls=%async_computation.2 | async-start | bytes 4194304 | tf_op jit(solution)/shard_map/all_to_all | solution.py:173

commit v2 on v1

v2 whole, which is shorter than its diff:
```python
import math

import jax
import jax.numpy as jnp
import numpy as np
from jax import lax
from jax.experimental import pallas as pl
from jax.experimental.pallas import tpu as pltpu
from jax.sharding import PartitionSpec as P

NT = 512
NF = 32
FLO = 4
BS = 8
ITERS = 5
CHUNKS = 4
AXES = ("row", "band")


def dft_tables():
    sample_index = np.arange(NT, dtype=np.int32)
    bin_index = FLO + np.arange(NF, dtype=np.int32)
    angles = (bin_index[:, None] * sample_index[None, :] % NT).astype(np.float32) * np.float32(
        2.0 * math.pi / NT
    )
    cycles = np.concatenate([np.cos(angles), -np.sin(angles)], axis=0)
    forward = cycles * np.float32(1.0 / math.sqrt(NT))
    inverse = cycles * np.float32(math.sqrt(2.0 / NF))
    return (jnp.asarray(forward, jnp.bfloat16), jnp.asarray(inverse, jnp.bfloat16))


def fill_kernel(
    partner_ref, wave_ref, data_ref, permute_ref, mask_ref, base_ref, factor_ref, turned, taken
):
    stations = data_ref.shape[1]
    block = min(128, stations)
    for part in range(2):

        @pl.loop(0, stations // block)
        def _(step):
            rows = pl.ds(pl.multiple_of(step * block, block), block)
            turned[:, rows] = data_ref[part, rows, :].astype(jnp.float32).T

        @pl.loop(0, stations // BS)
        def _(step):
            source = pl.ds(pl.multiple_of(partner_ref[step] * BS, BS), BS)
            into = pl.ds(pl.multiple_of(step * BS, BS), BS)
            taken[part, into, :] = turned[source, :]

    tile = min(256, stations)
    wave_re = wave_ref[0]
    wave_im = wave_ref[1]

    @pl.loop(0, stations // tile)
    def _(step):
        rows = pl.ds(pl.multiple_of(step * tile, tile), tile)
        lower = pl.ds(pl.multiple_of(stations + step * tile, tile), tile)
        present = mask_ref[rows, :].astype(jnp.float32) > 0.5
        filled = []
        for part in range(2):
            mirrored = jnp.dot(
                taken[part, rows, :].astype(jnp.bfloat16),
                permute_ref[...],
                preferred_element_type=jnp.float32,
            )
            value = jnp.where(present, data_ref[part, rows, :].astype(jnp.float32), mirrored)
            base_ref[rows, part * stations : (part + 1) * stations] = value.astype(jnp.bfloat16)
            filled.append(value)
        factor_re = (wave_re * filled[0] - wave_im * filled[1]).astype(jnp.bfloat16)
        factor_im = (wave_re * filled[1] + wave_im * filled[0]).astype(jnp.bfloat16)
        factor_ref[rows, :stations] = factor_re
        factor_ref[rows, stations:] = factor_im
        factor_ref[lower, :stations] = -factor_im
        factor_ref[lower, stations:] = factor_re


def fill(partner, wave, data, permute, mask):
    stations = data.shape[1]
    vmem = pl.BlockSpec(memory_space=pltpu.VMEM)
    smem = pl.BlockSpec(memory_space=pltpu.SMEM)
    return pl.pallas_call(
        fill_kernel,
        out_shape=(
            jax.ShapeDtypeStruct((stations, 2 * stations), jnp.bfloat16),
            jax.ShapeDtypeStruct((2 * stations, 2 * stations), jnp.bfloat16),
        ),
        in_specs=[smem, smem, vmem, vmem, vmem],
        out_specs=(vmem, vmem),
        scratch_shapes=[
            pltpu.VMEM((stations, stations), jnp.float32),
            pltpu.VMEM((2, stations, stations), jnp.float32),
        ],
        compiler_params=pltpu.CompilerParams(vmem_limit_bytes=56 << 20),
        cost_estimate=pl.CostEstimate(
            flops=4 * stations**3, bytes_accessed=20 * stations**2, transcendentals=0
        ),
        name="fill",
    )(partner, wave, data, permute, mask)


def solve_kernel(tile, base_ref, factor_ref, out_ref, held):
    width = base_ref.shape[1]
    half = width // 2
    for turn in range(ITERS):
        left = base_ref if turn == 0 else held.at[(turn + 1) % 2]

        @pl.loop(0, width // tile)
        def _(step):
            columns = pl.ds(pl.multiple_of(step * tile, tile), tile)
            product = jnp.dot(
                left[...], factor_ref[:, columns], preferred_element_type=jnp.float32
            )
            value = (base_ref[:, columns].astype(jnp.float32) - product).astype(jnp.bfloat16)
            if turn == ITERS - 1:
                inside = pl.ds(pl.multiple_of(step * tile % half, tile), tile)
                out_ref[step * tile // half, :, inside] = value
            else:
                held[turn % 2, :, columns] = value


def solve(base, factor):
    rows, width = base.shape
    tile = min(512, width // 2)
    vmem = pl.BlockSpec(memory_space=pltpu.VMEM)
    return pl.pallas_call(
        lambda *refs: solve_kernel(tile, *refs),
        out_shape=jax.ShapeDtypeStruct((2, rows, width // 2), jnp.bfloat16),
        in_specs=[vmem, vmem],
        out_specs=vmem,
        scratch_shapes=[pltpu.VMEM((2, rows, width), jnp.bfloat16)],
        compiler_params=pltpu.CompilerParams(vmem_limit_bytes=40 << 20),
        cost_estimate=pl.CostEstimate(
            flops=2 * ITERS * rows * width * width,
            bytes_accessed=2 * (2 * rows * width + width * width),
            transcendentals=0,
        ),
        name="solve",
    )(base, factor)


def restore_kernel(data_ref, table_ref, *rest):
    out_ref = rest[-1]
    for shot in range(data_ref.shape[0]):
        out_ref[shot] = lax.dot_general(
            data_ref[shot],
            table_ref[...],
            (((0,), (0,)), ((), ())),
            preferred_element_type=jnp.float32,
        ).astype(jnp.bfloat16)


def restore(data, table, whole, first, shot_count):
    count, parts, stations = data.shape
    samples = table.shape[1]
    step = math.gcd(math.gcd(4, count), first) if first else math.gcd(4, count)
    in_specs = [
        pl.BlockSpec((step, parts, stations), lambda i: (i, 0, 0)),
        pl.BlockSpec((parts, samples), lambda i: (0, 0)),
    ]
    args = [data, table]
    aliases = {}
    if whole is not None:
        in_specs.append(pl.BlockSpec(memory_space=pl.ANY))
        args.append(whole)
        aliases = {2: 0}
    return pl.pallas_call(
        restore_kernel,
        grid=(count // step,),
        out_shape=jax.ShapeDtypeStruct((shot_count, stations, samples), jnp.bfloat16),
        in_specs=in_specs,
        out_specs=pl.BlockSpec((step, stations, samples), lambda i: (first // step + i, 0, 0)),
        input_output_aliases=aliases,
        compiler_params=pltpu.CompilerParams(vmem_limit_bytes=32 << 20),
        cost_estimate=pl.CostEstimate(
            flops=2 * count * parts * stations * samples,
            bytes_accessed=2 * count * stations * (samples + parts),
            transcendentals=0,
        ),
        name="restore",
    )(*args)


def shards(recorded, acquired, partner, band_counts, wavelet):
    band_size = lax.axis_size("band")
    devices = band_size * lax.axis_size("row")
    shot_count, stations, _ = recorded.shape
    copies = devices // NF
    here = lax.axis_index("row") * band_size + lax.axis_index("band")
    forward, inverse = dft_tables()

    head = max(1, shot_count // 4)
    pieces = []
    for begin, end in ((0, head), (head, shot_count)):
        part = lax.slice_in_dim(recorded, begin, end, axis=0)
        spectra = jnp.einsum(
            "ct,srt->csr", forward, part, preferred_element_type=jnp.float32
        ).astype(jnp.bfloat16)
        spectra = jnp.swapaxes(spectra.reshape(2, NF, end - begin, stations), 0, 1)
        if copies > 1:
            spectra = jnp.repeat(spectra, copies, axis=0)
        pieces.append(lax.all_to_all(spectra, AXES, split_axis=0, concat_axis=0, tiled=True))
    data = jnp.concatenate(pieces, axis=2)
    data = jnp.swapaxes(data, 0, 1).reshape(2, stations, stations)

    offsets = jnp.arange(BS, dtype=jnp.int32)
    mirror_index = (BS * partner[:, None] + offsets[None, :]).reshape(stations)
    station = jnp.arange(stations, dtype=jnp.int32)
    permute = (station[:, None] == mirror_index[None, :]).astype(jnp.bfloat16)
    mask = jnp.repeat(jnp.repeat(acquired, BS, axis=0), BS, axis=1).astype(jnp.bfloat16)
    own_bin = here // copies
    own_group = jnp.sum((jnp.cumsum(band_counts) <= own_bin).astype(jnp.int32))
    chosen = jnp.arange(band_counts.shape[0], dtype=jnp.int32) == own_group
    rescale = 1.0 / math.sqrt(stations)
    wave = jnp.sum(chosen.astype(jnp.float32)[None] * wavelet, axis=1) * rescale
    base, factor = fill(partner, wave, data, permute, mask)

    own_count = shot_count // copies
    base = base.reshape(devices, shot_count, 2 * stations)
    if copies > 1:
        base = lax.dynamic_slice_in_dim(base, here % copies * own_count, own_count, axis=1)
    chunks = min(CHUNKS, own_count)
    size = own_count // chunks
    output = None
    for chunk in range(chunks):
        rows = lax.slice_in_dim(base, chunk * size, (chunk + 1) * size, axis=1)
        solved = solve(rows.reshape(devices * size, 2 * stations), factor)
        solved = jnp.swapaxes(solved.reshape(2, devices, size, stations), 0, 1)
        back = lax.all_to_all(solved, AXES, split_axis=0, concat_axis=0, tiled=True)
        if output is not None:
            back, output = lax.optimization_barrier((back, output))
        back = back.reshape(NF, copies, 2, size, stations)
        back = jnp.transpose(back, (1, 3, 2, 0, 4)).reshape(copies, size, 2 * NF, stations)
        for copy in range(copies):
            output = restore(
                back[copy], inverse, output, copy * own_count + chunk * size, shot_count
            )
    return output


def solution(mesh):
    return jax.shard_map(
        shards,
        mesh=mesh,
        in_specs=(P(AXES, None, None), P(), P(), P(), P()),
        out_specs=P(AXES, None, None),
        check_vma=False,
    )
```

time: 356 us -> 287 us (0.81); the launches traced: 350 us -> 286 us
  waiting for transfers between devices: 134 us -> 94.5 us
  other arithmetic: 44.3 us -> 6.2 us
  matrix products: 39.5 us -> 19.5 us
  local copies, waits for them, and re-layouts: 28.5 us -> 45.7 us
  Pallas kernels: 83.9 us -> 95.2 us
  starting transfers between devices: 17.7 us -> 24.9 us
    concatenate x2 -> x0, other arithmetic: 36.8 us -> none  [the longest x1 36.4 us: shards(): jnp.concatenate([jnp.concatenate([factor_re, factor_im], axis=1), jnp.con...]
    all_to_all x2 -> x4, waiting for transfers between devices: 59.5 us -> 28.9 us  [shards(): back = lax.all_to_all(solved, AXES, split_axis=0, concat_axis=0, tiled=True)]
    dot_general x2 -> x0, matrix products: 16.4 us -> none  [shards(): lax.dot_general(permute, moved.astype(jnp.bfloat16), (((1,), (1,)), ((),...]
    pallas_call x2 -> x5, Pallas kernels: 23.9 us -> 37.9 us  [the longest x1 19.1 us: fill(): pl.pallas_call(fill_kernel, out_shape=(jax.ShapeDtypeStruct((stations, 2...]
    unnamed x12 -> x22, local copies, waits for them, and re-layouts: 1.15 us -> 13.1 us
    all_to_all x2, waiting for transfers between devices: 74.5 us -> 65.6 us  [shards(): lax.all_to_all(spectra, AXES, split_axis=0, concat_axis=0, tiled=True)]
    all_to_all x2 -> x4, starting transfers between devices: 6.95 us -> 14.6 us  [shards(): back = lax.all_to_all(solved, AXES, split_axis=0, concat_axis=0, tiled=True)]
    convert_element_type x0 -> x4, local copies, waits for them, and re-layouts: none -> 7.42 us  [shards(): jnp.repeat(jnp.repeat(acquired, BS, axis=0), BS, axis=1)]
  transfers between devices with their start and end apart: 4 -> 6, of which waited for: 4 -> 6; matrix products, arithmetic and copies ran while one was open for 8% -> 14% of each run, Pallas kernels for 9% -> 20%
where the time goes in v2:
time: 287 us; the launch traced here: 286 us
  Pallas kernels  95.2 us (33%)
  waiting for transfers between devices  94.5 us (33%)
  local copies, waits for them, and re-layouts  45.7 us (16%)
  starting transfers between devices  24.9 us (9%)
  matrix products  19.5 us (7%)
  other arithmetic  6.2 us (2%)
    all_to_all x2, waiting for transfers between devices, shards(): lax.all_to_all(spectra, AXES, split_axis=0, concat_axis=0, tiled=True)  65.6 us
    pallas_call x4, Pallas kernels, solve(): pl.pallas_call(lambda *refs: solve_kernel(tile, *refs), out_shape=jax.Sha...  57.3 us
    all_to_all x4, waiting for transfers between devices, shards(): back = lax.all_to_all(solved, AXES, split_axis=0, concat_axis=0, tiled=True)  28.9 us
    dot_general x2, matrix products, shards(): jnp.einsum('ct,srt->csr', forward, part, preferred_element_type=jnp.float32)  19.5 us
    pallas_call x1, Pallas kernels, fill(): pl.pallas_call(fill_kernel, out_shape=(jax.ShapeDtypeStruct((stations, 2...  19.1 us
    pallas_call x4, Pallas kernels, restore(): pl.pallas_call(restore_kernel, grid=(count // step,), out_shape=jax.Shape...  18.8 us
    all_to_all x4, starting transfers between devices, shards(): back = lax.all_to_all(solved, AXES, split_axis=0, concat_axis=0, tiled=True)  14.6 us
    unnamed x22, local copies, waits for them, and re-layouts  13.1 us
  transfers between devices with their start and end apart: 6, of which 6 were waited for; matrix products, arithmetic and copies ran while one was open for 14% of the time, Pallas kernels for 20%

profile of v2, /device:TPU:1, one launch (start us, length us, event | category | flops | bytes accessed | tf_op | source)
XLA Modules:
  0.0 286.3 jit_solution(14873959543008905828)
XLA Ops:
  0.0 6.0 %fusion.8 = bf16[64,8,1024]{2,0,1:T(8,128)(2,1)S(1)} fusion(bf16[64,512,1]{1,0,2:T(8,128)(2,1)} %constant.38, bf16[32,1024,512]{2,1,0:T(8,128)(2,1)} %param.7), kind=kOutput, calls=%fused_computation.9 | convolution fusion | flops 537395200 | bytes 9502720 | tf_op jit(solution)/shard_map/ct,srt->csr/dot_general | solution.py:195
  7.6 7.1 %all-to-all-start = ((bf16[32,2,8,1024]{3,2,1,0:T(8,128)(2,1)}), bf16[32,2,8,1024]{3,2,1,0:T(8,128)(2,1)S(1)}, u32[]{:S(2)}, u32[]{:S(2)}) async-start(bf16[32,2,8,1024]{3,2,1,0:T(8,128)(2,1)} %bitcast.59), calls=%async_computation | async-start | bytes 2097152 | tf_op jit(solution)/shard_map/all_to_all | solution.py:201
  14.8 13.5 %fusion.5 = bf16[64,24,1024]{2,0,1:T(8,128)(2,1)} fusion(bf16[64,512,1]{1,0,2:T(8,128)(2,1)S(1)} %copy-done.10, bf16[32,1024,512]{2,1,0:T(8,128)(2,1)} %param.7), kind=kOutput, calls=%fused_computation.8 | convolution fusion | flops 1612185600 | bytes 28377088 | tf_op jit(solution)/shard_map/ct,srt->csr/dot_general | solution.py:195
  28.3 5.3 %copy.52 = bf16[2,32,24,1024]{3,2,0,1:T(8,128)(2,1)} copy(bf16[2,32,24,1024]{3,1,0,2:T(8,128)(2,1)} %bitcast.76) | data formatting | bytes 6291456 | tf_op jit(solution)/shard_map/reshape | solution.py:198
  33.5 7.6 %all-to-all-done = bf16[32,2,8,1024]{3,2,1,0:T(8,128)(2,1)S(1)} async-done(((bf16[32,2,8,1024]{3,2,1,0:T(8,128)(2,1)}), bf16[32,2,8,1024]{3,2,1,0:T(8,128)(2,1)S(1)}, u32[]{:S(2)}, u32[]{:S(2)}) %all-to-all-start) | async-done | bytes 1048608 | tf_op jit(solution)/shard_map/all_to_all | solution.py:201
  42.1 3.2 %all-to-all-start.1 = ((bf16[32,2,24,1024]{3,2,1,0:T(8,128)(2,1)}), bf16[32,2,24,1024]{3,2,1,0:T(8,128)(2,1)S(1)}, u32[]{:S(2)}, u32[]{:S(2)}) async-start(bf16[32,2,24,1024]{3,2,1,0:T(8,128)(2,1)} %bitcast.54), calls=%async_computation.1 | async-start | bytes 6291456 | tf_op jit(solution)/shard_map/all_to_all | solution.py:201
  49.0 3.9 %copy.37.mask_ref = bf16[1024,1024]{1,0:T(8,128)(2,1)} copy(bf16[1024,1024]{0,1:T(8,128)(2,1)} %broadcast_bitcast_fusion) | data formatting | bytes 4194304 | tf_op jit(solution)/shard_map/convert_element_type | solution.py:209
  55.2 2.3 fusion.4.permute_ref
  57.4 58.0 %all-to-all-done.1 = bf16[32,2,24,1024]{3,2,1,0:T(8,128)(2,1)S(1)} async-done(((bf16[32,2,24,1024]{3,2,1,0:T(8,128)(2,1)}), bf16[32,2,24,1024]{3,2,1,0:T(8,128)(2,1)S(1)}, u32[]{:S(2)}, u32[]{:S(2)}) %all-to-all-start.1) | async-done | bytes 3145760 | tf_op jit(solution)/shard_map/all_to_all | solution.py:201
  117.1 2.5 copy.35
  119.6 19.1 %fill.1 = (bf16[1024,2048]{1,0:T(8,128)(2,1)}, bf16[2048,2048]{1,0:T(8,128)(2,1)}) custom-call(s32[128]{0:T(128)} %partner_ref.1, f32[2]{0:T(128)} %broadcast_multiply_fusion.1.wave_ref, bf16[2,1024,1024]{2,1,0:T(8,128)(2,1)} %bitcast.69, bf16[1024,1024]{1,0:T(8,128)(2,1)} %fusion.4.permute_ref, bf16[1024,1024]{1,0:T(8,128)(2,1)} %copy.37.mask_ref), custom_call_target="tpu_custom_call" | custom-call | flops 4294967296 | bytes 20971520 | tf_op jit(solution)/shard_map/fill/pallas_call | solution.py:81
  138.8 2.7 slice_bitcast_fusion
  143.4 14.3 %solve.7 = bf16[2,256,1024]{2,1,0:T(8,128)(2,1)S(1)} custom-call(bf16[256,2048]{1,0:T(8,128)(2,1)S(1)} %get-tuple-element.21.refs_0_, bf16[2048,2048]{1,0:T(8,128)(2,1)S(1)} %copy-done.1), custom_call_target="tpu_custom_call" | custom-call | flops 10737418240 | bytes 10485760 | tf_op jit(solution)/shard_map/solve/pallas_call | solution.py:125
  159.8 4.9 %all-to-all-start.5 = ((bf16[32,2,8,1024]{3,1,2,0:T(2,128)(2,1)}), bf16[32,2,8,1024]{3,1,2,0:T(2,128)(2,1)}, u32[]{:S(2)}, u32[]{:S(2)}) async-start(bf16[32,2,8,1024]{3,1,2,0:T(2,128)(2,1)} %bitcast.75), calls=%async_computation.5 | async-start | bytes 2097152 | tf_op jit(solution)/shard_map/all_to_all | solution.py:228
  164.7 3.4 %copy-done.2 = bf16[2048,2048]{1,0:T(8,128)(2,1)S(1)} copy-done((bf16[2048,2048]{1,0:T(8,128)(2,1)S(1)}, bf16[2048,2048]{1,0:T(8,128)(2,1)}, u32[]{:S(2)}) %copy-start.2) | copy-done | bytes 8388632
  168.1 14.3 %solve.6 = bf16[2,256,1024]{2,1,0:T(8,128)(2,1)S(1)} custom-call(bf16[256,2048]{1,0:T(8,128)(2,1)S(1)} %get-tuple-element.22.refs_0_, bf16[2048,2048]{1,0:T(8,128)(2,1)S(1)} %copy-done.2), custom_call_target="tpu_custom_call" | custom-call | flops 10737418240 | bytes 10485760 | tf_op jit(solution)/shard_map/solve/pallas_call | solution.py:125
  184.5 6.6 %all-to-all-done.5 = bf16[32,2,8,1024]{3,1,2,0:T(2,128)(2,1)} async-done(((bf16[32,2,8,1024]{3,1,2,0:T(2,128)(2,1)}), bf16[32,2,8,1024]{3,1,2,0:T(2,128)(2,1)}, u32[]{:S(2)}, u32[]{:S(2)}) %all-to-all-start.5) | async-done | bytes 1048608 | tf_op jit(solution)/shard_map/all_to_all | solution.py:228
  191.1 3.2 %all-to-all-start.4 = ((bf16[32,2,8,1024]{3,1,2,0:T(2,128)(2,1)}), bf16[32,2,8,1024]{3,1,2,0:T(2,128)(2,1)S(1)}, u32[]{:S(2)}, u32[]{:S(2)}) async-start(bf16[32,2,8,1024]{3,1,2,0:T(2,128)(2,1)} %bitcast.74), calls=%async_computation.4 | async-start | bytes 2097152 | tf_op jit(solution)/shard_map/all_to_all | solution.py:228
  194.3 3.4 %copy-done.3 = bf16[2048,2048]{1,0:T(8,128)(2,1)S(1)} copy-done((bf16[2048,2048]{1,0:T(8,128)(2,1)S(1)}, bf16[2048,2048]{1,0:T(8,128)(2,1)}, u32[]{:S(2)}) %copy-start.3) | copy-done | bytes 8388632
  197.7 14.3 %solve.5 = bf16[2,256,1024]{2,1,0:T(8,128)(2,1)S(1)} custom-call(bf16[256,2048]{1,0:T(8,128)(2,1)S(1)} %get-tuple-element.23.refs_0_, bf16[2048,2048]{1,0:T(8,128)(2,1)S(1)} %copy-done.3), custom_call_target="tpu_custom_call" | custom-call | flops 10737418240 | bytes 10485760 | tf_op jit(solution)/shard_map/solve/pallas_call | solution.py:125
  214.0 6.6 %all-to-all-done.4 = bf16[32,2,8,1024]{3,1,2,0:T(2,128)(2,1)S(1)} async-done(((bf16[32,2,8,1024]{3,1,2,0:T(2,128)(2,1)}), bf16[32,2,8,1024]{3,1,2,0:T(2,128)(2,1)S(1)}, u32[]{:S(2)}, u32[]{:S(2)}) %all-to-all-start.4) | async-done | bytes 1048608 | tf_op jit(solution)/shard_map/all_to_all | solution.py:228
  220.6 3.2 %all-to-all-start.3 = ((bf16[32,2,8,1024]{3,1,2,0:T(2,128)(2,1)}), bf16[32,2,8,1024]{3,1,2,0:T(2,128)(2,1)S(1)}, u32[]{:S(2)}, u32[]{:S(2)}) async-start(bf16[32,2,8,1024]{3,1,2,0:T(2,128)(2,1)} %bitcast.73), calls=%async_computation.3 | async-start | bytes 2097152 | tf_op jit(solution)/shard_map/all_to_all | solution.py:228
  223.8 3.4 %copy-done.4 = bf16[2048,2048]{1,0:T(8,128)(2,1)S(1)} copy-done((bf16[2048,2048]{1,0:T(8,128)(2,1)S(1)}, bf16[2048,2048]{1,0:T(8,128)(2,1)}, u32[]{:S(2)}) %copy-start.4) | copy-done | bytes 8388632
  227.2 14.3 %solve.4 = bf16[2,256,1024]{2,1,0:T(8,128)(2,1)S(1)} custom-call(bf16[256,2048]{1,0:T(8,128)(2,1)S(1)} %get-tuple-element.24.refs_0_, bf16[2048,2048]{1,0:T(8,128)(2,1)S(1)} %copy-done.4), custom_call_target="tpu_custom_call" | custom-call | flops 10737418240 | bytes 10485760 | tf_op jit(solution)/shard_map/solve/pallas_call | solution.py:125
  241.5 2.1 copy.56
  243.6 6.6 %all-to-all-done.3 = bf16[32,2,8,1024]{3,1,2,0:T(2,128)(2,1)S(1)} async-done(((bf16[32,2,8,1024]{3,1,2,0:T(2,128)(2,1)}), bf16[32,2,8,1024]{3,1,2,0:T(2,128)(2,1)S(1)}, u32[]{:S(2)}, u32[]{:S(2)}) %all-to-all-start.3) | async-done | bytes 1048608 | tf_op jit(solution)/shard_map/all_to_all | solution.py:228
  250.1 3.4 %all-to-all-start.2 = ((bf16[32,2,8,1024]{3,1,2,0:T(2,128)(2,1)}), bf16[32,2,8,1024]{3,1,2,0:T(2,128)(2,1)}, u32[]{:S(2)}, u32[]{:S(2)}) async-start(bf16[32,2,8,1024]{3,1,2,0:T(2,128)(2,1)} %bitcast.72), calls=%async_computation.2 | async-start | bytes 2097152 | tf_op jit(solution)/shard_map/all_to_all | solution.py:228
  255.4 4.7 %restore.4.rest_0_ = bf16[32,1024,512]{2,1,0:T(8,128)(2,1)} custom-call(bf16[8,64,1024]{2,1,0:T(8,128)(2,1)S(1)} %bitcast.63, bf16[64,512]{1,0:T(8,128)(2,1)S(1)} %copy-done), custom_call_target="tpu_custom_call" | custom-call | flops 536870912 | bytes 9437184 | tf_op jit(solution)/shard_map/restore/pallas_call | solution.py:166
  260.6 4.7 %restore.5.rest_0_ = bf16[32,1024,512]{2,1,0:T(8,128)(2,1)} custom-call(bf16[8,64,1024]{2,1,0:T(8,128)(2,1)S(1)} %bitcast.61, bf16[64,512]{1,0:T(8,128)(2,1)S(1)} %copy-done, bf16[32,1024,512]{2,1,0:T(8,128)(2,1)} %restore.4.rest_0_), custom_call_target="tpu_custom_call", output_to_operand_aliasing={{}: (2, {})} | custom-call | flops 536870912 | bytes 9437184 | tf_op jit(solution)/shard_map/restore/pallas_call | solution.py:166
  265.9 4.7 %restore.6.rest_0_ = bf16[32,1024,512]{2,1,0:T(8,128)(2,1)} custom-call(bf16[8,64,1024]{2,1,0:T(8,128)(2,1)S(1)} %bitcast.62, bf16[64,512]{1,0:T(8,128)(2,1)S(1)} %copy-done, bf16[32,1024,512]{2,1,0:T(8,128)(2,1)} %restore.5.rest_0_), custom_call_target="tpu_custom_call", output_to_operand_aliasing={{}: (2, {})} | custom-call | flops 536870912 | bytes 9437184 | tf_op jit(solution)/shard_map/restore/pallas_call | solution.py:166
  270.6 9.1 %all-to-all-done.2 = bf16[32,2,8,1024]{3,1,2,0:T(2,128)(2,1)} async-done(((bf16[32,2,8,1024]{3,1,2,0:T(2,128)(2,1)}), bf16[32,2,8,1024]{3,1,2,0:T(2,128)(2,1)}, u32[]{:S(2)}, u32[]{:S(2)}) %all-to-all-start.2) | async-done | bytes 1048608 | tf_op jit(solution)/shard_map/all_to_all | solution.py:228
  281.6 4.7 %restore.7 = bf16[32,1024,512]{2,1,0:T(8,128)(2,1)} custom-call(bf16[8,64,1024]{2,1,0:T(8,128)(2,1)S(1)} %bitcast.60, bf16[64,512]{1,0:T(8,128)(2,1)S(1)} %copy-done, bf16[32,1024,512]{2,1,0:T(8,128)(2,1)} %restore.6.rest_0_), custom_call_target="tpu_custom_call", output_to_operand_aliasing={{}: (2, {})} | custom-call | flops 536870912 | bytes 9437184 | tf_op jit(solution)/shard_map/restore/pallas_call | solution.py:166
  (40 shorter events, 23.0 us)
Async XLA Ops:
  6.0 8.7 %copy-start.10 = (bf16[64,512,1]{1,0,2:T(8,128)(2,1)S(1)}, bf16[64,512,1]{1,0,2:T(8,128)(2,1)}, u32[]{:S(2)}) copy-start(bf16[64,512,1]{1,0,2:T(8,128)(2,1)} %constant.38) | copy-start | bytes 196612
  7.6 33.5 %all-to-all-start = ((bf16[32,2,8,1024]{3,2,1,0:T(8,128)(2,1)}), bf16[32,2,8,1024]{3,2,1,0:T(8,128)(2,1)S(1)}, u32[]{:S(2)}, u32[]{:S(2)}) async-start(bf16[32,2,8,1024]{3,2,1,0:T(8,128)(2,1)} %bitcast.59), calls=%async_computation | async-start | bytes 2097152 | tf_op jit(solution)/shard_map/all_to_all | solution.py:201
  33.5 11.8 %copy-start.6 = (s32[128,128]{1,0:T(8,128)S(1)}, s32[128,128]{1,0:T(8,128)}, u32[]{:S(2)}) copy-start(s32[128,128]{1,0:T(8,128)} %param.8) | copy-start | bytes 196612
  33.5 11.8 %copy-start.9 = (s32[128]{0:T(128)S(1)}, s32[128]{0:T(128)}, u32[]{:S(2)}) copy-start(s32[128]{0:T(128)} %partner_ref.1) | copy-start | bytes 1540
  41.1 1.0 copy-start.5
  42.1 73.3 %all-to-all-start.1 = ((bf16[32,2,24,1024]{3,2,1,0:T(8,128)(2,1)}), bf16[32,2,24,1024]{3,2,1,0:T(8,128)(2,1)S(1)}, u32[]{:S(2)}, u32[]{:S(2)}) async-start(bf16[32,2,24,1024]{3,2,1,0:T(8,128)(2,1)} %bitcast.54), calls=%async_computation.1 | async-start | bytes 6291456 | tf_op jit(solution)/shard_map/all_to_all | solution.py:201
  45.3 7.7 %copy-start.8 = (s32[4]{0:T(128)S(1)}, s32[4]{0:T(128)}, u32[]{:S(2)}) copy-start(s32[4]{0:T(128)} %param.10) | copy-start | bytes 52
  45.3 9.1 %copy-start.7 = (f32[2,4]{1,0:T(2,128)S(1)}, f32[2,4]{1,0:T(2,128)}, u32[]{:S(2)}) copy-start(f32[2,4]{1,0:T(2,128)} %param.11) | copy-start | bytes 100
  138.8 4.7 %copy-start.1 = (bf16[2048,2048]{1,0:T(8,128)(2,1)S(1)}, bf16[2048,2048]{1,0:T(8,128)(2,1)}, u32[]{:S(2)}) copy-start(bf16[2048,2048]{1,0:T(8,128)(2,1)} %get-tuple-element.14.refs_1_) | copy-start | bytes 25165828
  159.8 31.3 %all-to-all-start.5 = ((bf16[32,2,8,1024]{3,1,2,0:T(2,128)(2,1)}), bf16[32,2,8,1024]{3,1,2,0:T(2,128)(2,1)}, u32[]{:S(2)}, u32[]{:S(2)}) async-start(bf16[32,2,8,1024]{3,1,2,0:T(2,128)(2,1)} %bitcast.75), calls=%async_computation.5 | async-start | bytes 2097152 | tf_op jit(solution)/shard_map/all_to_all | solution.py:228
  164.7 3.4 %copy-start.2 = (bf16[2048,2048]{1,0:T(8,128)(2,1)S(1)}, bf16[2048,2048]{1,0:T(8,128)(2,1)}, u32[]{:S(2)}) copy-start(bf16[2048,2048]{1,0:T(8,128)(2,1)} %get-tuple-element.14.refs_1_) | copy-start | bytes 25165828
  191.1 29.5 %all-to-all-start.4 = ((bf16[32,2,8,1024]{3,1,2,0:T(2,128)(2,1)}), bf16[32,2,8,1024]{3,1,2,0:T(2,128)(2,1)S(1)}, u32[]{:S(2)}, u32[]{:S(2)}) async-start(bf16[32,2,8,1024]{3,1,2,0:T(2,128)(2,1)} %bitcast.74), calls=%async_computation.4 | async-start | bytes 2097152 | tf_op jit(solution)/shard_map/all_to_all | solution.py:228
  194.3 3.4 %copy-start.3 = (bf16[2048,2048]{1,0:T(8,128)(2,1)S(1)}, bf16[2048,2048]{1,0:T(8,128)(2,1)}, u32[]{:S(2)}) copy-start(bf16[2048,2048]{1,0:T(8,128)(2,1)} %get-tuple-element.14.refs_1_) | copy-start | bytes 25165828
  220.6 29.5 %all-to-all-start.3 = ((bf16[32,2,8,1024]{3,1,2,0:T(2,128)(2,1)}), bf16[32,2,8,1024]{3,1,2,0:T(2,128)(2,1)S(1)}, u32[]{:S(2)}, u32[]{:S(2)}) async-start(bf16[32,2,8,1024]{3,1,2,0:T(2,128)(2,1)} %bitcast.73), calls=%async_computation.3 | async-start | bytes 2097152 | tf_op jit(solution)/shard_map/all_to_all | solution.py:228
  223.8 3.4 %copy-start.4 = (bf16[2048,2048]{1,0:T(8,128)(2,1)S(1)}, bf16[2048,2048]{1,0:T(8,128)(2,1)}, u32[]{:S(2)}) copy-start(bf16[2048,2048]{1,0:T(8,128)(2,1)} %get-tuple-element.14.refs_1_) | copy-start | bytes 25165828
  241.5 13.8 %copy-start = (bf16[64,512]{1,0:T(8,128)(2,1)S(1)}, bf16[64,512]{1,0:T(8,128)(2,1)}, u32[]{:S(2)}) copy-start(bf16[64,512]{1,0:T(8,128)(2,1)} %constant.37.clone.table_ref) | copy-start | bytes 196612
  250.1 29.6 %all-to-all-start.2 = ((bf16[32,2,8,1024]{3,1,2,0:T(2,128)(2,1)}), bf16[32,2,8,1024]{3,1,2,0:T(2,128)(2,1)}, u32[]{:S(2)}, u32[]{:S(2)}) async-start(bf16[32,2,8,1024]{3,1,2,0:T(2,128)(2,1)} %bitcast.72), calls=%async_computation.2 | async-start | bytes 2097152 | tf_op jit(solution)/shard_map/all_to_all | solution.py:228

commit v3 on v2

--- a/solution.py
+++ b/solution.py
@@ -29,11 +29,44 @@
     return (jnp.asarray(forward, jnp.bfloat16), jnp.asarray(inverse, jnp.bfloat16))
 
 
-def fill_kernel(
-    partner_ref, wave_ref, data_ref, permute_ref, mask_ref, base_ref, factor_ref, turned, taken
-):
+def iterate(tile, base_ref, factor_ref, out_ref, held):
+    width = base_ref.shape[1]
+    half = width // 2
+    for turn in range(ITERS):
+        left = base_ref if turn == 0 else held.at[(turn + 1) % 2]
+
+        @pl.loop(0, width // tile)
+        def _(step):
+            columns = pl.ds(pl.multiple_of(step * tile, tile), tile)
+            product = jnp.dot(
+                left[...], factor_ref[:, columns], preferred_element_type=jnp.float32
+            )
+            value = base_ref[:, columns].astype(jnp.float32) - product
+            if turn == ITERS - 1:
+                inside = pl.ds(pl.multiple_of(step * tile % half, tile), tile)
+                part = step * tile // half
+                if len(out_ref.shape) == 4:
+                    groups, _, size, _ = out_ref.shape
+                    value = value.reshape(groups, size, tile)
+                    out_ref[:, part, :, inside] = value.astype(jnp.bfloat16)
+                else:
+                    out_ref[part, :, inside] = value.astype(jnp.bfloat16)
+            else:
+                held[turn % 2, :, columns] = value.astype(jnp.bfloat16)
+
+
+def fill_kernel(shots, chunks, tile, *refs):
+    partner_ref, wave_ref, data_ref, permute_hbm, mask_hbm = refs[:5]
+    base_hbm, factor_hbm = refs[5:7]
+    out_ref = refs[7] if chunks > 1 else None
+    refs = refs[8 if chunks > 1 else 7 :]
+    turned, taken, permute_ref, mask_ref, base_ref, factor_ref, held, sems = refs
     stations = data_ref.shape[1]
     block = min(128, stations)
+    load_permute = pltpu.make_async_copy(permute_hbm, permute_ref, sems.at[0])
+    load_mask = pltpu.make_async_copy(mask_hbm, mask_ref, sems.at[1])
+    load_permute.start()
+    load_mask.start()
     for part in range(2):
 
         @pl.loop(0, stations // block)
@@ -41,31 +74,46 @@
             rows = pl.ds(pl.multiple_of(step * block, block), block)
             turned[:, rows] = data_ref[part, rows, :].astype(jnp.float32).T
 
-        @pl.loop(0, stations // BS)
+        @pl.loop(0, stations // (4 * BS))
         def _(step):
-            source = pl.ds(pl.multiple_of(partner_ref[step] * BS, BS), BS)
-            into = pl.ds(pl.multiple_of(step * BS, BS), BS)
-            taken[part, into, :] = turned[source, :]
-
-    tile = min(256, stations)
+            for inner in range(4):
+                source = pl.ds(pl.multiple_of(partner_ref[4 * step + inner] * BS, BS), BS)
+                into = pl.ds(pl.multiple_of((4 * step + inner) * BS, BS), BS)
+                taken[part, into, :] = turned[source, :]
+
+    load_permute.wait()
+    load_mask.wait()
+    high = min(256, stations)
+    size = shots // chunks
+    piece = high // chunks
     wave_re = wave_ref[0]
     wave_im = wave_ref[1]
 
-    @pl.loop(0, stations // tile)
+    @pl.loop(0, stations // high)
     def _(step):
-        rows = pl.ds(pl.multiple_of(step * tile, tile), tile)
-        lower = pl.ds(pl.multiple_of(stations + step * tile, tile), tile)
+        rows = pl.ds(pl.multiple_of(step * high, high), high)
+        lower = pl.ds(pl.multiple_of(stations + step * high, high), high)
+        pieces = pl.ds(pl.multiple_of(step * piece, piece), piece)
         present = mask_ref[rows, :].astype(jnp.float32) > 0.5
         filled = []
         for part in range(2):
+            columns = slice(part * stations, (part + 1) * stations)
             mirrored = jnp.dot(
                 taken[part, rows, :].astype(jnp.bfloat16),
                 permute_ref[...],
                 preferred_element_type=jnp.float32,
             )
             value = jnp.where(present, data_ref[part, rows, :].astype(jnp.float32), mirrored)
-            base_ref[rows, part * stations : (part + 1) * stations] = value.astype(jnp.bfloat16)
             filled.append(value)
+            if chunks > 1:
+                grouped = value.reshape(high // shots, shots, stations)
+                for chunk in range(chunks):
+                    own = grouped[:, chunk * size : (chunk + 1) * size]
+                    base_ref[chunk, pieces, columns] = own.reshape(piece, stations).astype(
+                        jnp.bfloat16
+                    )
+            else:
+                base_ref[0, rows, columns] = value.astype(jnp.bfloat16)
         factor_re = (wave_re * filled[0] - wave_im * filled[1]).astype(jnp.bfloat16)
         factor_im = (wave_re * filled[1] + wave_im * filled[0]).astype(jnp.bfloat16)
         factor_ref[rows, :stations] = factor_re
@@ -73,22 +121,46 @@
         factor_ref[lower, :stations] = -factor_im
         factor_ref[lower, stations:] = factor_re
 
-
-def fill(partner, wave, data, permute, mask):
+    store_base = pltpu.make_async_copy(base_ref, base_hbm, sems.at[2])
+    store_factor = pltpu.make_async_copy(factor_ref, factor_hbm, sems.at[3])
+    store_base.start()
+    store_factor.start()
+    if chunks > 1:
+        iterate(tile, base_ref.at[0], factor_ref, out_ref, held)
+    store_base.wait()
+    store_factor.wait()
+
+
+def fill(partner, wave, data, permute, mask, shots, chunks):
     stations = data.shape[1]
+    rows = stations // chunks
+    width = 2 * stations
     vmem = pl.BlockSpec(memory_space=pltpu.VMEM)
     smem = pl.BlockSpec(memory_space=pltpu.SMEM)
+    hbm = pl.BlockSpec(memory_space=pl.ANY)
+    out_shape = [
+        jax.ShapeDtypeStruct((chunks, rows, width), jnp.bfloat16),
+        jax.ShapeDtypeStruct((width, width), jnp.bfloat16),
+    ]
+    if chunks > 1:
+        size = shots // chunks
+        out_shape.append(
+            jax.ShapeDtypeStruct((stations // shots, 2, size, stations), jnp.bfloat16)
+        )
     return pl.pallas_call(
-        fill_kernel,
-        out_shape=(
-            jax.ShapeDtypeStruct((stations, 2 * stations), jnp.bfloat16),
-            jax.ShapeDtypeStruct((2 * stations, 2 * stations), jnp.bfloat16),
-        ),
-        in_specs=[smem, smem, vmem, vmem, vmem],
-        out_specs=(vmem, vmem),
+        lambda *refs: fill_kernel(shots, chunks, min(512, stations), *refs),
+        out_shape=out_shape,
+        in_specs=[smem, smem, vmem, hbm, hbm],
+        out_specs=[hbm, hbm, vmem][: len(out_shape)],
         scratch_shapes=[
             pltpu.VMEM((stations, stations), jnp.float32),
             pltpu.VMEM((2, stations, stations), jnp.float32),
+            pltpu.VMEM((stations, stations), jnp.bfloat16),
+            pltpu.VMEM((stations, stations), jnp.bfloat16),
+            pltpu.VMEM((chunks, rows, width), jnp.bfloat16),
+            pltpu.VMEM((width, width), jnp.bfloat16),
+            pltpu.VMEM((2, rows if chunks > 1 else 16, width), jnp.bfloat16),
+            pltpu.SemaphoreType.DMA((4,)),
         ],
         compiler_params=pltpu.CompilerParams(vmem_limit_bytes=56 << 20),
         cost_estimate=pl.CostEstimate(
@@ -99,34 +171,23 @@
 
 
 def solve_kernel(tile, base_ref, factor_ref, out_ref, held):
-    width = base_ref.shape[1]
-    half = width // 2
-    for turn in range(ITERS):
-        left = base_ref if turn == 0 else held.at[(turn + 1) % 2]
-
-        @pl.loop(0, width // tile)
-        def _(step):
-            columns = pl.ds(pl.multiple_of(step * tile, tile), tile)
-            product = jnp.dot(
-                left[...], factor_ref[:, columns], preferred_element_type=jnp.float32
-            )
-            value = (base_ref[:, columns].astype(jnp.float32) - product).astype(jnp.bfloat16)
-            if turn == ITERS - 1:
-                inside = pl.ds(pl.multiple_of(step * tile % half, tile), tile)
-                out_ref[step * tile // half, :, inside] = value
-            else:
-                held[turn % 2, :, columns] = value
-
-
-def solve(base, factor):
-    rows, width = base.shape
-    tile = min(512, width // 2)
-    vmem = pl.BlockSpec(memory_space=pltpu.VMEM)
-    return pl.pallas_call(
-        lambda *refs: solve_kernel(tile, *refs),
-        out_shape=jax.ShapeDtypeStruct((2, rows, width // 2), jnp.bfloat16),
-        in_specs=[vmem, vmem],
-        out_specs=vmem,
+    iterate(tile, base_ref, factor_ref, out_ref, held)
+
+
+def solve(base, factor, chunk, groups):
+    _, rows, width = base.shape
+    stations = width // 2
+    size = rows // groups
+    shape = (groups, 2, size, stations) if size % 8 == 0 else (2, rows, stations)
+    solved = pl.pallas_call(
+        lambda *refs: solve_kernel(min(512, stations), *refs),
+        grid=(1,),
+        out_shape=jax.ShapeDtypeStruct(shape, jnp.bfloat16),
+        in_specs=[
+            pl.BlockSpec((None, rows, width), lambda i: (chunk, 0, 0)),
+            pl.BlockSpec((width, width), lambda i: (0, 0), pipeline_mode=pl.Buffered(1)),
+        ],
+        out_specs=pl.BlockSpec(shape, lambda i: (0,) * len(shape)),
         scratch_shapes=[pltpu.VMEM((2, rows, width), jnp.bfloat16)],
         compiler_params=pltpu.CompilerParams(vmem_limit_bytes=40 << 20),
         cost_estimate=pl.CostEstimate(
@@ -136,6 +197,9 @@
         ),
         name="solve",
     )(base, factor)
+    if len(shape) == 3:
+        solved = jnp.swapaxes(solved.reshape(2, groups, size, stations), 0, 1)
+    return solved
 
 
 def restore_kernel(data_ref, table_ref, *rest):
@@ -212,19 +276,23 @@
     chosen = jnp.arange(band_counts.shape[0], dtype=jnp.int32) == own_group
     rescale = 1.0 / math.sqrt(stations)
     wave = jnp.sum(chosen.astype(jnp.float32)[None] * wavelet, axis=1) * rescale
-    base, factor = fill(partner, wave, data, permute, mask)
-
     own_count = shot_count // copies
-    base = base.reshape(devices, shot_count, 2 * stations)
-    if copies > 1:
-        base = lax.dynamic_slice_in_dim(base, here % copies * own_count, own_count, axis=1)
     chunks = min(CHUNKS, own_count)
     size = own_count // chunks
+    together = copies == 1 and size % 8 == 0 and chunks > 1
+    made = fill(partner, wave, data, permute, mask, shot_count, chunks if together else 1)
+    base, factor = made[:2]
+    if not together:
+        base = base.reshape(devices, shot_count, 2 * stations)
+        base = lax.dynamic_slice_in_dim(base, here % copies * own_count, own_count, axis=1)
+        base = jnp.swapaxes(base.reshape(devices, chunks, size, 2 * stations), 0, 1)
+        base = base.reshape(chunks, devices * size, 2 * stations)
     output = None
     for chunk in range(chunks):
-        rows = lax.slice_in_dim(base, chunk * size, (chunk + 1) * size, axis=1)
-        solved = solve(rows.reshape(devices * size, 2 * stations), factor)
-        solved = jnp.swapaxes(solved.reshape(2, devices, size, stations), 0, 1)
+        if together and chunk == 0:
+            solved = made[2]
+        else:
+            solved = solve(base, factor, chunk, devices)
         back = lax.all_to_all(solved, AXES, split_axis=0, concat_axis=0, tiled=True)
         if output is not None:
             back, output = lax.optimization_barrier((back, output))

time: 287 us -> 275 us (0.958)
  local copies, waits for them, and re-layouts: 45.7 us -> 38.1 us
  Pallas kernels: 95.2 us -> 92.2 us
    reshape x5 -> x0, local copies, waits for them, and re-layouts: 11 us -> none  [the longest x4 8.24 us: shards(): solved = jnp.swapaxes(solved.reshape(2, devices, size, stations), 0, 1)]
    unnamed x22 -> x26, local copies, waits for them, and re-layouts: 13.1 us -> 17.7 us
    pallas_call x5 -> x4, Pallas kernels: 76.4 us -> 73.3 us  [the longest x3 45.9 us: solve(): pl.pallas_call(lambda *refs: solve_kernel(min(512, stations), *refs), gri...]
  transfers between devices with their start and end apart: 6 -> 6, of which waited for: 6 -> 6; matrix products, arithmetic and copies ran while one was open for 14% -> 12% of each run, Pallas kernels for 20% -> 22%
where the time goes in v3:
time: 275 us; the launch traced here: 273 us
  waiting for transfers between devices  92.5 us (34%)
  Pallas kernels  92.2 us (34%)
  local copies, waits for them, and re-layouts  38.1 us (14%)
  starting transfers between devices  24.7 us (9%)
  matrix products  19.5 us (7%)
  other arithmetic  6.2 us (2%)
    all_to_all x2, waiting for transfers between devices, shards(): lax.all_to_all(spectra, AXES, split_axis=0, concat_axis=0, tiled=True)  65.6 us
    pallas_call x3, Pallas kernels, solve(): pl.pallas_call(lambda *refs: solve_kernel(min(512, stations), *refs), gri...  45.9 us
    pallas_call x1, Pallas kernels, fill(): pl.pallas_call(lambda *refs: fill_kernel(shots, chunks, min(512, stations...  27.4 us
    all_to_all x4, waiting for transfers between devices, shards(): back = lax.all_to_all(solved, AXES, split_axis=0, concat_axis=0, tiled=True)  26.9 us
    dot_general x2, matrix products, shards(): jnp.einsum('ct,srt->csr', forward, part, preferred_element_type=jnp.float32)  19.5 us
    pallas_call x4, Pallas kernels, restore(): pl.pallas_call(restore_kernel, grid=(count // step,), out_shape=jax.Shape...  18.8 us
    unnamed x26, local copies, waits for them, and re-layouts  17.7 us
    all_to_all x4, starting transfers between devices, shards(): back = lax.all_to_all(solved, AXES, split_axis=0, concat_axis=0, tiled=True)  14.4 us
  transfers between devices with their start and end apart: 6, of which 6 were waited for; matrix products, arithmetic and copies ran while one was open for 12% of the time, Pallas kernels for 22%

profile of v3, /device:TPU:1, one launch (start us, length us, event | category | flops | bytes accessed | tf_op | source)
XLA Modules:
  0.0 273.5 jit_solution(3732711369038170436)
XLA Ops:
  0.0 6.0 %fusion.8 = bf16[64,8,1024]{2,0,1:T(8,128)(2,1)S(1)} fusion(bf16[64,512,1]{1,0,2:T(8,128)(2,1)} %constant.38, bf16[32,1024,512]{2,1,0:T(8,128)(2,1)} %param.7), kind=kOutput, calls=%fused_computation.9 | convolution fusion | flops 537395200 | bytes 9502720 | tf_op jit(solution)/shard_map/ct,srt->csr/dot_general | solution.py:259
  7.6 7.1 %all-to-all-start = ((bf16[32,2,8,1024]{3,2,1,0:T(8,128)(2,1)}), bf16[32,2,8,1024]{3,2,1,0:T(8,128)(2,1)S(1)}, u32[]{:S(2)}, u32[]{:S(2)}) async-start(bf16[32,2,8,1024]{3,2,1,0:T(8,128)(2,1)} %bitcast.34), calls=%async_computation | async-start | bytes 2097152 | tf_op jit(solution)/shard_map/all_to_all | solution.py:265
  14.8 13.5 %fusion.5 = bf16[64,24,1024]{2,0,1:T(8,128)(2,1)} fusion(bf16[64,512,1]{1,0,2:T(8,128)(2,1)S(1)} %copy-done.12, bf16[32,1024,512]{2,1,0:T(8,128)(2,1)} %param.7), kind=kOutput, calls=%fused_computation.8 | convolution fusion | flops 1612185600 | bytes 28377088 | tf_op jit(solution)/shard_map/ct,srt->csr/dot_general | solution.py:259
  28.3 5.3 %copy.44 = bf16[2,32,24,1024]{3,2,0,1:T(8,128)(2,1)} copy(bf16[2,32,24,1024]{3,1,0,2:T(8,128)(2,1)} %bitcast.43) | data formatting | bytes 6291456 | tf_op jit(solution)/shard_map/reshape | solution.py:262
  33.5 7.6 %all-to-all-done = bf16[32,2,8,1024]{3,2,1,0:T(8,128)(2,1)S(1)} async-done(((bf16[32,2,8,1024]{3,2,1,0:T(8,128)(2,1)}), bf16[32,2,8,1024]{3,2,1,0:T(8,128)(2,1)S(1)}, u32[]{:S(2)}, u32[]{:S(2)}) %all-to-all-start) | async-done | bytes 1048608 | tf_op jit(solution)/shard_map/all_to_all | solution.py:265
  42.1 3.2 %all-to-all-start.1 = ((bf16[32,2,24,1024]{3,2,1,0:T(8,128)(2,1)}), bf16[32,2,24,1024]{3,2,1,0:T(8,128)(2,1)S(1)}, u32[]{:S(2)}, u32[]{:S(2)}) async-start(bf16[32,2,24,1024]{3,2,1,0:T(8,128)(2,1)} %bitcast.33), calls=%async_computation.1 | async-start | bytes 6291456 | tf_op jit(solution)/shard_map/all_to_all | solution.py:265
  49.0 3.9 %copy.37.refs_4_ = bf16[1024,1024]{1,0:T(8,128)(2,1)} copy(bf16[1024,1024]{0,1:T(8,128)(2,1)} %broadcast_bitcast_fusion) | data formatting | bytes 4194304 | tf_op jit(solution)/shard_map/convert_element_type | solution.py:273
  55.1 2.3 fusion.4.refs_3_
  57.4 58.0 %all-to-all-done.1 = bf16[32,2,24,1024]{3,2,1,0:T(8,128)(2,1)S(1)} async-done(((bf16[32,2,24,1024]{3,2,1,0:T(8,128)(2,1)}), bf16[32,2,24,1024]{3,2,1,0:T(8,128)(2,1)S(1)}, u32[]{:S(2)}, u32[]{:S(2)}) %all-to-all-start.1) | async-done | bytes 3145760 | tf_op jit(solution)/shard_map/all_to_all | solution.py:265
  117.1 2.5 copy.35
  119.6 27.4 %fill.1 = (bf16[4,256,2048]{2,1,0:T(8,128)(2,1)}, bf16[2048,2048]{1,0:T(8,128)(2,1)}, bf16[32,2,8,1024]{3,2,1,0:T(8,128)(2,1)}) custom-call(s32[128]{0:T(128)} %refs_0_.1, f32[2]{0:T(128)} %broadcast_multiply_fusion.1.refs_1_, bf16[2,1024,1024]{2,1,0:T(8,128)(2,1)} %bitcast.39, bf16[1024,1024]{1,0:T(8,128)(2,1)} %fusion.4.refs_3_, ...), custom_call_target="tpu_custom_call" | custom-call | flops 4294967296 | bytes 20971520 | tf_op jit(solution)/shard_map/fill/pallas_call | solution.py:150
  147.0 4.9 %all-to-all-start.5 = ((bf16[32,2,8,1024]{3,2,1,0:T(8,128)(2,1)}), bf16[32,2,8,1024]{3,2,1,0:T(8,128)(2,1)S(1)}, u32[]{:S(2)}, u32[]{:S(2)}) async-start(bf16[32,2,8,1024]{3,2,1,0:T(8,128)(2,1)} %get-tuple-element.16), calls=%async_computation.5 | async-start | bytes 2097152 | tf_op jit(solution)/shard_map/all_to_all | solution.py:296
  152.0 3.4 %copy-done.1 = bf16[2048,2048]{1,0:T(8,128)(2,1)S(1)} copy-done((bf16[2048,2048]{1,0:T(8,128)(2,1)S(1)}, bf16[2048,2048]{1,0:T(8,128)(2,1)}, u32[]{:S(2)}) %copy-start.1) | copy-done | bytes 8388632
  155.3 2.2 copy-done.4
  157.5 15.3 %solve.5 = bf16[32,2,8,1024]{3,2,1,0:T(8,128)(2,1)} custom-call(bf16[4,256,2048]{2,1,0:T(8,128)(2,1)S(1)} %copy-done.4, bf16[2048,2048]{1,0:T(8,128)(2,1)S(1)} %copy-done.1), custom_call_target="tpu_custom_call" | custom-call | flops 10737418240 | bytes 10485760 | tf_op jit(solution)/shard_map/solve/pallas_call | solution.py:182
  172.9 5.4 %all-to-all-done.5 = bf16[32,2,8,1024]{3,2,1,0:T(8,128)(2,1)S(1)} async-done(((bf16[32,2,8,1024]{3,2,1,0:T(8,128)(2,1)}), bf16[32,2,8,1024]{3,2,1,0:T(8,128)(2,1)S(1)}, u32[]{:S(2)}, u32[]{:S(2)}) %all-to-all-start.5) | async-done | bytes 1048608 | tf_op jit(solution)/shard_map/all_to_all | solution.py:296
  178.3 3.2 %all-to-all-start.4 = ((bf16[32,2,8,1024]{3,2,1,0:T(8,128)(2,1)}), bf16[32,2,8,1024]{3,2,1,0:T(8,128)(2,1)S(1)}, u32[]{:S(2)}, u32[]{:S(2)}) async-start(bf16[32,2,8,1024]{3,2,1,0:T(8,128)(2,1)} %solve.5), calls=%async_computation.4 | async-start | bytes 2097152 | tf_op jit(solution)/shard_map/all_to_all | solution.py:296
  181.5 3.4 %copy-done.2 = bf16[2048,2048]{1,0:T(8,128)(2,1)S(1)} copy-done((bf16[2048,2048]{1,0:T(8,128)(2,1)S(1)}, bf16[2048,2048]{1,0:T(8,128)(2,1)}, u32[]{:S(2)}) %copy-start.2) | copy-done | bytes 8388632
  184.9 2.2 copy-done.5
  187.0 15.3 %solve.4 = bf16[32,2,8,1024]{3,2,1,0:T(8,128)(2,1)} custom-call(bf16[4,256,2048]{2,1,0:T(8,128)(2,1)S(1)} %copy-done.5, bf16[2048,2048]{1,0:T(8,128)(2,1)S(1)} %copy-done.2), custom_call_target="tpu_custom_call" | custom-call | flops 10737418240 | bytes 10485760 | tf_op jit(solution)/shard_map/solve/pallas_call | solution.py:182
  202.3 5.5 %all-to-all-done.4 = bf16[32,2,8,1024]{3,2,1,0:T(8,128)(2,1)S(1)} async-done(((bf16[32,2,8,1024]{3,2,1,0:T(8,128)(2,1)}), bf16[32,2,8,1024]{3,2,1,0:T(8,128)(2,1)S(1)}, u32[]{:S(2)}, u32[]{:S(2)}) %all-to-all-start.4) | async-done | bytes 1048608 | tf_op jit(solution)/shard_map/all_to_all | solution.py:296
  207.8 3.2 %all-to-all-start.3 = ((bf16[32,2,8,1024]{3,2,1,0:T(8,128)(2,1)}), bf16[32,2,8,1024]{3,2,1,0:T(8,128)(2,1)S(1)}, u32[]{:S(2)}, u32[]{:S(2)}) async-start(bf16[32,2,8,1024]{3,2,1,0:T(8,128)(2,1)} %solve.4), calls=%async_computation.3 | async-start | bytes 2097152 | tf_op jit(solution)/shard_map/all_to_all | solution.py:296
  211.0 3.4 %copy-done.3 = bf16[2048,2048]{1,0:T(8,128)(2,1)S(1)} copy-done((bf16[2048,2048]{1,0:T(8,128)(2,1)S(1)}, bf16[2048,2048]{1,0:T(8,128)(2,1)}, u32[]{:S(2)}) %copy-start.3) | copy-done | bytes 8388632
  214.4 2.2 copy-done.6
  216.6 15.3 %solve.3 = bf16[32,2,8,1024]{3,2,1,0:T(8,128)(2,1)} custom-call(bf16[4,256,2048]{2,1,0:T(8,128)(2,1)S(1)} %copy-done.6, bf16[2048,2048]{1,0:T(8,128)(2,1)S(1)} %copy-done.3), custom_call_target="tpu_custom_call" | custom-call | flops 10737418240 | bytes 10485760 | tf_op jit(solution)/shard_map/solve/pallas_call | solution.py:182
  231.9 5.5 %all-to-all-done.3 = bf16[32,2,8,1024]{3,2,1,0:T(8,128)(2,1)S(1)} async-done(((bf16[32,2,8,1024]{3,2,1,0:T(8,128)(2,1)}), bf16[32,2,8,1024]{3,2,1,0:T(8,128)(2,1)S(1)}, u32[]{:S(2)}, u32[]{:S(2)}) %all-to-all-start.3) | async-done | bytes 1048608 | tf_op jit(solution)/shard_map/all_to_all | solution.py:296
  237.3 3.2 %all-to-all-start.2 = ((bf16[32,2,8,1024]{3,2,1,0:T(8,128)(2,1)}), bf16[32,2,8,1024]{3,2,1,0:T(8,128)(2,1)}, u32[]{:S(2)}, u32[]{:S(2)}) async-start(bf16[32,2,8,1024]{3,2,1,0:T(8,128)(2,1)} %solve.3), calls=%async_computation.2 | async-start | bytes 2097152 | tf_op jit(solution)/shard_map/all_to_all | solution.py:296
  241.2 4.7 %restore.4.rest_0_ = bf16[32,1024,512]{2,1,0:T(8,128)(2,1)} custom-call(bf16[8,64,1024]{2,1,0:T(8,128)(2,1)S(1)} %bitcast.38, bf16[64,512]{1,0:T(8,128)(2,1)S(1)} %copy-done), custom_call_target="tpu_custom_call" | custom-call | flops 536870912 | bytes 9437184 | tf_op jit(solution)/shard_map/restore/pallas_call | solution.py:230
  246.4 4.7 %restore.5.rest_0_ = bf16[32,1024,512]{2,1,0:T(8,128)(2,1)} custom-call(bf16[8,64,1024]{2,1,0:T(8,128)(2,1)S(1)} %bitcast.36, bf16[64,512]{1,0:T(8,128)(2,1)S(1)} %copy-done, bf16[32,1024,512]{2,1,0:T(8,128)(2,1)} %restore.4.rest_0_), custom_call_target="tpu_custom_call", output_to_operand_aliasing={{}: (2, {})} | custom-call | flops 536870912 | bytes 9437184 | tf_op jit(solution)/shard_map/restore/pallas_call | solution.py:230
  251.7 4.7 %restore.6.rest_0_ = bf16[32,1024,512]{2,1,0:T(8,128)(2,1)} custom-call(bf16[8,64,1024]{2,1,0:T(8,128)(2,1)S(1)} %bitcast.37, bf16[64,512]{1,0:T(8,128)(2,1)S(1)} %copy-done, bf16[32,1024,512]{2,1,0:T(8,128)(2,1)} %restore.5.rest_0_), custom_call_target="tpu_custom_call", output_to_operand_aliasing={{}: (2, {})} | custom-call | flops 536870912 | bytes 9437184 | tf_op jit(solution)/shard_map/restore/pallas_call | solution.py:230
  256.4 10.5 %all-to-all-done.2 = bf16[32,2,8,1024]{3,2,1,0:T(8,128)(2,1)} async-done(((bf16[32,2,8,1024]{3,2,1,0:T(8,128)(2,1)}), bf16[32,2,8,1024]{3,2,1,0:T(8,128)(2,1)}, u32[]{:S(2)}, u32[]{:S(2)}) %all-to-all-start.2) | async-done | bytes 1048608 | tf_op jit(solution)/shard_map/all_to_all | solution.py:296
  268.8 4.7 %restore.7 = bf16[32,1024,512]{2,1,0:T(8,128)(2,1)} custom-call(bf16[8,64,1024]{2,1,0:T(8,128)(2,1)S(1)} %bitcast.35, bf16[64,512]{1,0:T(8,128)(2,1)S(1)} %copy-done, bf16[32,1024,512]{2,1,0:T(8,128)(2,1)} %restore.6.rest_0_), custom_call_target="tpu_custom_call", output_to_operand_aliasing={{}: (2, {})} | custom-call | flops 536870912 | bytes 9437184 | tf_op jit(solution)/shard_map/restore/pallas_call | solution.py:230
  (38 shorter events, 13.7 us)
Async XLA Ops:
  6.0 8.7 %copy-start.12 = (bf16[64,512,1]{1,0,2:T(8,128)(2,1)S(1)}, bf16[64,512,1]{1,0,2:T(8,128)(2,1)}, u32[]{:S(2)}) copy-start(bf16[64,512,1]{1,0,2:T(8,128)(2,1)} %constant.38) | copy-start | bytes 196612
  7.6 33.5 %all-to-all-start = ((bf16[32,2,8,1024]{3,2,1,0:T(8,128)(2,1)}), bf16[32,2,8,1024]{3,2,1,0:T(8,128)(2,1)S(1)}, u32[]{:S(2)}, u32[]{:S(2)}) async-start(bf16[32,2,8,1024]{3,2,1,0:T(8,128)(2,1)} %bitcast.34), calls=%async_computation | async-start | bytes 2097152 | tf_op jit(solution)/shard_map/all_to_all | solution.py:265
  33.5 11.8 %copy-start.8 = (s32[128,128]{1,0:T(8,128)S(1)}, s32[128,128]{1,0:T(8,128)}, u32[]{:S(2)}) copy-start(s32[128,128]{1,0:T(8,128)} %param.8) | copy-start | bytes 196612
  33.5 11.8 %copy-start.11 = (s32[128]{0:T(128)S(1)}, s32[128]{0:T(128)}, u32[]{:S(2)}) copy-start(s32[128]{0:T(128)} %refs_0_.1) | copy-start | bytes 1540
  41.1 1.0 copy-start.7
  42.1 73.3 %all-to-all-start.1 = ((bf16[32,2,24,1024]{3,2,1,0:T(8,128)(2,1)}), bf16[32,2,24,1024]{3,2,1,0:T(8,128)(2,1)S(1)}, u32[]{:S(2)}, u32[]{:S(2)}) async-start(bf16[32,2,24,1024]{3,2,1,0:T(8,128)(2,1)} %bitcast.33), calls=%async_computation.1 | async-start | bytes 6291456 | tf_op jit(solution)/shard_map/all_to_all | solution.py:265
  45.3 7.7 %copy-start.10 = (s32[4]{0:T(128)S(1)}, s32[4]{0:T(128)}, u32[]{:S(2)}) copy-start(s32[4]{0:T(128)} %param.10) | copy-start | bytes 52
  45.3 9.1 %copy-start.9 = (f32[2,4]{1,0:T(2,128)S(1)}, f32[2,4]{1,0:T(2,128)}, u32[]{:S(2)}) copy-start(f32[2,4]{1,0:T(2,128)} %param.11) | copy-start | bytes 100
  147.0 31.3 %all-to-all-start.5 = ((bf16[32,2,8,1024]{3,2,1,0:T(8,128)(2,1)}), bf16[32,2,8,1024]{3,2,1,0:T(8,128)(2,1)S(1)}, u32[]{:S(2)}, u32[]{:S(2)}) async-start(bf16[32,2,8,1024]{3,2,1,0:T(8,128)(2,1)} %get-tuple-element.16), calls=%async_computation.5 | async-start | bytes 2097152 | tf_op jit(solution)/shard_map/all_to_all | solution.py:296
  152.0 3.4 %copy-start.1 = (bf16[2048,2048]{1,0:T(8,128)(2,1)S(1)}, bf16[2048,2048]{1,0:T(8,128)(2,1)}, u32[]{:S(2)}) copy-start(bf16[2048,2048]{1,0:T(8,128)(2,1)} %get-tuple-element.15.refs_1_) | copy-start | bytes 25165828
  155.3 2.2 copy-start.4
  178.3 29.5 %all-to-all-start.4 = ((bf16[32,2,8,1024]{3,2,1,0:T(8,128)(2,1)}), bf16[32,2,8,1024]{3,2,1,0:T(8,128)(2,1)S(1)}, u32[]{:S(2)}, u32[]{:S(2)}) async-start(bf16[32,2,8,1024]{3,2,1,0:T(8,128)(2,1)} %solve.5), calls=%async_computation.4 | async-start | bytes 2097152 | tf_op jit(solution)/shard_map/all_to_all | solution.py:296
  181.5 3.4 %copy-start.2 = (bf16[2048,2048]{1,0:T(8,128)(2,1)S(1)}, bf16[2048,2048]{1,0:T(8,128)(2,1)}, u32[]{:S(2)}) copy-start(bf16[2048,2048]{1,0:T(8,128)(2,1)} %get-tuple-element.15.refs_1_) | copy-start | bytes 25165828
  184.9 2.2 copy-start.5
  207.8 29.5 %all-to-all-start.3 = ((bf16[32,2,8,1024]{3,2,1,0:T(8,128)(2,1)}), bf16[32,2,8,1024]{3,2,1,0:T(8,128)(2,1)S(1)}, u32[]{:S(2)}, u32[]{:S(2)}) async-start(bf16[32,2,8,1024]{3,2,1,0:T(8,128)(2,1)} %solve.4), calls=%async_computation.3 | async-start | bytes 2097152 | tf_op jit(solution)/shard_map/all_to_all | solution.py:296
  211.0 3.4 %copy-start.3 = (bf16[2048,2048]{1,0:T(8,128)(2,1)S(1)}, bf16[2048,2048]{1,0:T(8,128)(2,1)}, u32[]{:S(2)}) copy-start(bf16[2048,2048]{1,0:T(8,128)(2,1)} %get-tuple-element.15.refs_1_) | copy-start | bytes 25165828
  214.4 2.2 copy-start.6
  231.9 9.3 %copy-start = (bf16[64,512]{1,0:T(8,128)(2,1)S(1)}, bf16[64,512]{1,0:T(8,128)(2,1)}, u32[]{:S(2)}) copy-start(bf16[64,512]{1,0:T(8,128)(2,1)} %constant.37.clone.table_ref) | copy-start | bytes 196612
  237.3 29.6 %all-to-all-start.2 = ((bf16[32,2,8,1024]{3,2,1,0:T(8,128)(2,1)}), bf16[32,2,8,1024]{3,2,1,0:T(8,128)(2,1)}, u32[]{:S(2)}, u32[]{:S(2)}) async-start(bf16[32,2,8,1024]{3,2,1,0:T(8,128)(2,1)} %solve.3), calls=%async_computation.2 | async-start | bytes 2097152 | tf_op jit(solution)/shard_map/all_to_all | solution.py:296

commit v4 on v3

--- a/solution.py
+++ b/solution.py
@@ -55,13 +55,19 @@
                 held[turn % 2, :, columns] = value.astype(jnp.bfloat16)
 
 
+def source_rows(data_ref, part, step, count):
+    shots, stations = data_ref.shape[2:]
+    sources = pl.ds(step * (count // shots), count // shots)
+    return data_ref[sources, part].astype(jnp.float32).reshape(count, stations)
+
+
 def fill_kernel(shots, chunks, tile, *refs):
     partner_ref, wave_ref, data_ref, permute_hbm, mask_hbm = refs[:5]
     base_hbm, factor_hbm = refs[5:7]
     out_ref = refs[7] if chunks > 1 else None
     refs = refs[8 if chunks > 1 else 7 :]
     turned, taken, permute_ref, mask_ref, base_ref, factor_ref, held, sems = refs
-    stations = data_ref.shape[1]
+    stations = data_ref.shape[3]
     block = min(128, stations)
     load_permute = pltpu.make_async_copy(permute_hbm, permute_ref, sems.at[0])
     load_mask = pltpu.make_async_copy(mask_hbm, mask_ref, sems.at[1])
@@ -72,7 +78,7 @@
         @pl.loop(0, stations // block)
         def _(step):
             rows = pl.ds(pl.multiple_of(step * block, block), block)
-            turned[:, rows] = data_ref[part, rows, :].astype(jnp.float32).T
+            turned[:, rows] = source_rows(data_ref, part, step, block).T
 
         @pl.loop(0, stations // (4 * BS))
         def _(step):
@@ -103,7 +109,7 @@
                 permute_ref[...],
                 preferred_element_type=jnp.float32,
             )
-            value = jnp.where(present, data_ref[part, rows, :].astype(jnp.float32), mirrored)
+            value = jnp.where(present, source_rows(data_ref, part, step, high), mirrored)
             filled.append(value)
             if chunks > 1:
                 grouped = value.reshape(high // shots, shots, stations)
@@ -132,7 +138,7 @@
 
 
 def fill(partner, wave, data, permute, mask, shots, chunks):
-    stations = data.shape[1]
+    stations = data.shape[3]
     rows = stations // chunks
     width = 2 * stations
     vmem = pl.BlockSpec(memory_space=pltpu.VMEM)
@@ -264,7 +270,6 @@
             spectra = jnp.repeat(spectra, copies, axis=0)
         pieces.append(lax.all_to_all(spectra, AXES, split_axis=0, concat_axis=0, tiled=True))
     data = jnp.concatenate(pieces, axis=2)
-    data = jnp.swapaxes(data, 0, 1).reshape(2, stations, stations)
 
     offsets = jnp.arange(BS, dtype=jnp.int32)
     mirror_index = (BS * partner[:, None] + offsets[None, :]).reshape(stations)

time: 275 us -> 274 us (level)
    concatenate x0 -> x1, other arithmetic: none -> 3.78 us  [shards(): data = jnp.concatenate(pieces, axis=2)]
where the time goes in v4:
time: 274 us; the launch traced here: 273 us
  waiting for transfers between devices  92.5 us (34%)
  Pallas kernels  92.2 us (34%)
  local copies, waits for them, and re-layouts  35.7 us (13%)
  starting transfers between devices  24.6 us (9%)
  matrix products  19.6 us (7%)
  other arithmetic  8.28 us (3%)
    all_to_all x2, waiting for transfers between devices, shards(): lax.all_to_all(spectra, AXES, split_axis=0, concat_axis=0, tiled=True)  65.6 us
    pallas_call x3, Pallas kernels, solve(): pl.pallas_call(lambda *refs: solve_kernel(min(512, stations), *refs), gri...  45.9 us
    pallas_call x1, Pallas kernels, fill(): pl.pallas_call(lambda *refs: fill_kernel(shots, chunks, min(512, stations...  27.4 us
    all_to_all x4, waiting for transfers between devices, shards(): back = lax.all_to_all(solved, AXES, split_axis=0, concat_axis=0, tiled=True)  26.9 us
    dot_general x2, matrix products, shards(): jnp.einsum('ct,srt->csr', forward, part, preferred_element_type=jnp.float32)  19.6 us
    pallas_call x4, Pallas kernels, restore(): pl.pallas_call(restore_kernel, grid=(count // step,), out_shape=jax.Shape...  18.8 us
    unnamed x26, local copies, waits for them, and re-layouts  17.7 us
    all_to_all x4, starting transfers between devices, shards(): back = lax.all_to_all(solved, AXES, split_axis=0, concat_axis=0, tiled=True)  14.4 us
  transfers between devices with their start and end apart: 6, of which 6 were waited for; matrix products, arithmetic and copies ran while one was open for 12% of the time, Pallas kernels for 22%

profile of v4, /device:TPU:1, one launch (start us, length us, event | category | flops | bytes accessed | tf_op | source)
XLA Modules:
  0.0 273.1 jit_solution(1736690027929744083)
XLA Ops:
  0.0 6.1 %fusion.8 = bf16[64,8,1024]{2,0,1:T(8,128)(2,1)S(1)} fusion(bf16[64,512,1]{1,0,2:T(8,128)(2,1)} %constant.38, bf16[32,1024,512]{2,1,0:T(8,128)(2,1)} %param.7), kind=kOutput, calls=%fused_computation.9 | convolution fusion | flops 537395200 | bytes 9502720 | tf_op jit(solution)/shard_map/ct,srt->csr/dot_general | solution.py:265
  7.7 7.1 %all-to-all-start = ((bf16[32,2,8,1024]{3,2,1,0:T(8,128)(2,1)}), bf16[32,2,8,1024]{3,2,1,0:T(8,128)(2,1)S(1)}, u32[]{:S(2)}, u32[]{:S(2)}) async-start(bf16[32,2,8,1024]{3,2,1,0:T(8,128)(2,1)} %bitcast.31), calls=%async_computation | async-start | bytes 2097152 | tf_op jit(solution)/shard_map/all_to_all | solution.py:271
  14.8 13.5 %fusion.5 = bf16[64,24,1024]{2,0,1:T(8,128)(2,1)} fusion(bf16[64,512,1]{1,0,2:T(8,128)(2,1)S(1)} %copy-done.12, bf16[32,1024,512]{2,1,0:T(8,128)(2,1)} %param.7), kind=kOutput, calls=%fused_computation.8 | convolution fusion | flops 1612185600 | bytes 28377088 | tf_op jit(solution)/shard_map/ct,srt->csr/dot_general | solution.py:265
  28.3 5.3 %copy.41 = bf16[2,32,24,1024]{3,2,0,1:T(8,128)(2,1)} copy(bf16[2,32,24,1024]{3,1,0,2:T(8,128)(2,1)} %bitcast.39) | data formatting | bytes 6291456 | tf_op jit(solution)/shard_map/reshape | solution.py:268
  33.6 7.5 %all-to-all-done = bf16[32,2,8,1024]{3,2,1,0:T(8,128)(2,1)S(1)} async-done(((bf16[32,2,8,1024]{3,2,1,0:T(8,128)(2,1)}), bf16[32,2,8,1024]{3,2,1,0:T(8,128)(2,1)S(1)}, u32[]{:S(2)}, u32[]{:S(2)}) %all-to-all-start) | async-done | bytes 1048608 | tf_op jit(solution)/shard_map/all_to_all | solution.py:271
  42.1 3.2 %all-to-all-start.1 = ((bf16[32,2,24,1024]{3,2,1,0:T(8,128)(2,1)}), bf16[32,2,24,1024]{3,2,1,0:T(8,128)(2,1)S(1)}, u32[]{:S(2)}, u32[]{:S(2)}) async-start(bf16[32,2,24,1024]{3,2,1,0:T(8,128)(2,1)} %bitcast.30), calls=%async_computation.1 | async-start | bytes 6291456 | tf_op jit(solution)/shard_map/all_to_all | solution.py:271
  49.0 3.9 %copy.30.refs_4_ = bf16[1024,1024]{1,0:T(8,128)(2,1)} copy(bf16[1024,1024]{0,1:T(8,128)(2,1)} %broadcast_bitcast_fusion) | data formatting | bytes 4194304 | tf_op jit(solution)/shard_map/convert_element_type | solution.py:278
  55.1 2.3 fusion.4.refs_3_
  57.4 58.0 %all-to-all-done.1 = bf16[32,2,24,1024]{3,2,1,0:T(8,128)(2,1)S(1)} async-done(((bf16[32,2,24,1024]{3,2,1,0:T(8,128)(2,1)}), bf16[32,2,24,1024]{3,2,1,0:T(8,128)(2,1)S(1)}, u32[]{:S(2)}, u32[]{:S(2)}) %all-to-all-start.1) | async-done | bytes 3145760 | tf_op jit(solution)/shard_map/all_to_all | solution.py:271
  115.5 3.8 %pad_maximum_fusion.refs_2_ = bf16[32,2,32,1024]{3,2,1,0:T(8,128)(2,1)} fusion(bf16[32,2,24,1024]{3,2,1,0:T(8,128)(2,1)S(1)} %all-to-all-done.1, bf16[32,2,8,1024]{3,2,1,0:T(8,128)(2,1)} %copy-done.7), kind=kLoop, calls=%fused_computation.4 | loop fusion | flops 8388608 | bytes 8388608 | tf_op jit(solution)/shard_map/concatenate | solution.py:272
  119.2 27.4 %fill.1 = (bf16[4,256,2048]{2,1,0:T(8,128)(2,1)}, bf16[2048,2048]{1,0:T(8,128)(2,1)}, bf16[32,2,8,1024]{3,2,1,0:T(8,128)(2,1)}) custom-call(s32[128]{0:T(128)} %refs_0_.1, f32[2]{0:T(128)} %broadcast_multiply_fusion.1.refs_1_, bf16[32,2,32,1024]{3,2,1,0:T(8,128)(2,1)} %pad_maximum_fusion.refs_2_, bf16[1024,1024]{1,0:T(8,128)(2,1)} %fusion.4.refs_3_, ...), custom_call_target="tpu_custom_call" | custom-call | flops 4294967296 | bytes 20971520 | tf_op jit(solution)/shard_map/fill/pallas_call | solution.py:156
  146.7 4.9 %all-to-all-start.5 = ((bf16[32,2,8,1024]{3,2,1,0:T(8,128)(2,1)}), bf16[32,2,8,1024]{3,2,1,0:T(8,128)(2,1)S(1)}, u32[]{:S(2)}, u32[]{:S(2)}) async-start(bf16[32,2,8,1024]{3,2,1,0:T(8,128)(2,1)} %get-tuple-element.16), calls=%async_computation.5 | async-start | bytes 2097152 | tf_op jit(solution)/shard_map/all_to_all | solution.py:301
  151.5 3.4 %copy-done.1 = bf16[2048,2048]{1,0:T(8,128)(2,1)S(1)} copy-done((bf16[2048,2048]{1,0:T(8,128)(2,1)S(1)}, bf16[2048,2048]{1,0:T(8,128)(2,1)}, u32[]{:S(2)}) %copy-start.1) | copy-done | bytes 8388632
  154.9 2.2 copy-done.4
  157.1 15.3 %solve.5 = bf16[32,2,8,1024]{3,2,1,0:T(8,128)(2,1)} custom-call(bf16[4,256,2048]{2,1,0:T(8,128)(2,1)S(1)} %copy-done.4, bf16[2048,2048]{1,0:T(8,128)(2,1)S(1)} %copy-done.1), custom_call_target="tpu_custom_call" | custom-call | flops 10737418240 | bytes 10485760 | tf_op jit(solution)/shard_map/solve/pallas_call | solution.py:188
  172.4 5.4 %all-to-all-done.5 = bf16[32,2,8,1024]{3,2,1,0:T(8,128)(2,1)S(1)} async-done(((bf16[32,2,8,1024]{3,2,1,0:T(8,128)(2,1)}), bf16[32,2,8,1024]{3,2,1,0:T(8,128)(2,1)S(1)}, u32[]{:S(2)}, u32[]{:S(2)}) %all-to-all-start.5) | async-done | bytes 1048608 | tf_op jit(solution)/shard_map/all_to_all | solution.py:301
  177.9 3.2 %all-to-all-start.4 = ((bf16[32,2,8,1024]{3,2,1,0:T(8,128)(2,1)}), bf16[32,2,8,1024]{3,2,1,0:T(8,128)(2,1)S(1)}, u32[]{:S(2)}, u32[]{:S(2)}) async-start(bf16[32,2,8,1024]{3,2,1,0:T(8,128)(2,1)} %solve.5), calls=%async_computation.4 | async-start | bytes 2097152 | tf_op jit(solution)/shard_map/all_to_all | solution.py:301
  181.1 3.4 %copy-done.2 = bf16[2048,2048]{1,0:T(8,128)(2,1)S(1)} copy-done((bf16[2048,2048]{1,0:T(8,128)(2,1)S(1)}, bf16[2048,2048]{1,0:T(8,128)(2,1)}, u32[]{:S(2)}) %copy-start.2) | copy-done | bytes 8388632
  184.4 2.2 copy-done.5
  186.6 15.3 %solve.4 = bf16[32,2,8,1024]{3,2,1,0:T(8,128)(2,1)} custom-call(bf16[4,256,2048]{2,1,0:T(8,128)(2,1)S(1)} %copy-done.5, bf16[2048,2048]{1,0:T(8,128)(2,1)S(1)} %copy-done.2), custom_call_target="tpu_custom_call" | custom-call | flops 10737418240 | bytes 10485760 | tf_op jit(solution)/shard_map/solve/pallas_call | solution.py:188
  201.9 5.5 %all-to-all-done.4 = bf16[32,2,8,1024]{3,2,1,0:T(8,128)(2,1)S(1)} async-done(((bf16[32,2,8,1024]{3,2,1,0:T(8,128)(2,1)}), bf16[32,2,8,1024]{3,2,1,0:T(8,128)(2,1)S(1)}, u32[]{:S(2)}, u32[]{:S(2)}) %all-to-all-start.4) | async-done | bytes 1048608 | tf_op jit(solution)/shard_map/all_to_all | solution.py:301
  207.4 3.2 %all-to-all-start.3 = ((bf16[32,2,8,1024]{3,2,1,0:T(8,128)(2,1)}), bf16[32,2,8,1024]{3,2,1,0:T(8,128)(2,1)S(1)}, u32[]{:S(2)}, u32[]{:S(2)}) async-start(bf16[32,2,8,1024]{3,2,1,0:T(8,128)(2,1)} %solve.4), calls=%async_computation.3 | async-start | bytes 2097152 | tf_op jit(solution)/shard_map/all_to_all | solution.py:301
  210.6 3.4 %copy-done.3 = bf16[2048,2048]{1,0:T(8,128)(2,1)S(1)} copy-done((bf16[2048,2048]{1,0:T(8,128)(2,1)S(1)}, bf16[2048,2048]{1,0:T(8,128)(2,1)}, u32[]{:S(2)}) %copy-start.3) | copy-done | bytes 8388632
  214.0 2.2 copy-done.6
  216.2 15.3 %solve.3 = bf16[32,2,8,1024]{3,2,1,0:T(8,128)(2,1)} custom-call(bf16[4,256,2048]{2,1,0:T(8,128)(2,1)S(1)} %copy-done.6, bf16[2048,2048]{1,0:T(8,128)(2,1)S(1)} %copy-done.3), custom_call_target="tpu_custom_call" | custom-call | flops 10737418240 | bytes 10485760 | tf_op jit(solution)/shard_map/solve/pallas_call | solution.py:188
  231.5 5.5 %all-to-all-done.3 = bf16[32,2,8,1024]{3,2,1,0:T(8,128)(2,1)S(1)} async-done(((bf16[32,2,8,1024]{3,2,1,0:T(8,128)(2,1)}), bf16[32,2,8,1024]{3,2,1,0:T(8,128)(2,1)S(1)}, u32[]{:S(2)}, u32[]{:S(2)}) %all-to-all-start.3) | async-done | bytes 1048608 | tf_op jit(solution)/shard_map/all_to_all | solution.py:301
  236.9 3.2 %all-to-all-start.2 = ((bf16[32,2,8,1024]{3,2,1,0:T(8,128)(2,1)}), bf16[32,2,8,1024]{3,2,1,0:T(8,128)(2,1)}, u32[]{:S(2)}, u32[]{:S(2)}) async-start(bf16[32,2,8,1024]{3,2,1,0:T(8,128)(2,1)} %solve.3), calls=%async_computation.2 | async-start | bytes 2097152 | tf_op jit(solution)/shard_map/all_to_all | solution.py:301
  240.7 4.7 %restore.4.rest_0_ = bf16[32,1024,512]{2,1,0:T(8,128)(2,1)} custom-call(bf16[8,64,1024]{2,1,0:T(8,128)(2,1)S(1)} %bitcast.35, bf16[64,512]{1,0:T(8,128)(2,1)S(1)} %copy-done), custom_call_target="tpu_custom_call" | custom-call | flops 536870912 | bytes 9437184 | tf_op jit(solution)/shard_map/restore/pallas_call | solution.py:236
  246.0 4.7 %restore.5.rest_0_ = bf16[32,1024,512]{2,1,0:T(8,128)(2,1)} custom-call(bf16[8,64,1024]{2,1,0:T(8,128)(2,1)S(1)} %bitcast.33, bf16[64,512]{1,0:T(8,128)(2,1)S(1)} %copy-done, bf16[32,1024,512]{2,1,0:T(8,128)(2,1)} %restore.4.rest_0_), custom_call_target="tpu_custom_call", output_to_operand_aliasing={{}: (2, {})} | custom-call | flops 536870912 | bytes 9437184 | tf_op jit(solution)/shard_map/restore/pallas_call | solution.py:236
  251.3 4.7 %restore.6.rest_0_ = bf16[32,1024,512]{2,1,0:T(8,128)(2,1)} custom-call(bf16[8,64,1024]{2,1,0:T(8,128)(2,1)S(1)} %bitcast.34, bf16[64,512]{1,0:T(8,128)(2,1)S(1)} %copy-done, bf16[32,1024,512]{2,1,0:T(8,128)(2,1)} %restore.5.rest_0_), custom_call_target="tpu_custom_call", output_to_operand_aliasing={{}: (2, {})} | custom-call | flops 536870912 | bytes 9437184 | tf_op jit(solution)/shard_map/restore/pallas_call | solution.py:236
  256.0 10.5 %all-to-all-done.2 = bf16[32,2,8,1024]{3,2,1,0:T(8,128)(2,1)} async-done(((bf16[32,2,8,1024]{3,2,1,0:T(8,128)(2,1)}), bf16[32,2,8,1024]{3,2,1,0:T(8,128)(2,1)}, u32[]{:S(2)}, u32[]{:S(2)}) %all-to-all-start.2) | async-done | bytes 1048608 | tf_op jit(solution)/shard_map/all_to_all | solution.py:301
  268.4 4.7 %restore.7 = bf16[32,1024,512]{2,1,0:T(8,128)(2,1)} custom-call(bf16[8,64,1024]{2,1,0:T(8,128)(2,1)S(1)} %bitcast.32, bf16[64,512]{1,0:T(8,128)(2,1)S(1)} %copy-done, bf16[32,1024,512]{2,1,0:T(8,128)(2,1)} %restore.6.rest_0_), custom_call_target="tpu_custom_call", output_to_operand_aliasing={{}: (2, {})} | custom-call | flops 536870912 | bytes 9437184 | tf_op jit(solution)/shard_map/restore/pallas_call | solution.py:236
  (37 shorter events, 12.0 us)
Async XLA Ops:
  0.0 14.8 %copy-start.12 = (bf16[64,512,1]{1,0,2:T(8,128)(2,1)S(1)}, bf16[64,512,1]{1,0,2:T(8,128)(2,1)}, u32[]{:S(2)}) copy-start(bf16[64,512,1]{1,0,2:T(8,128)(2,1)} %constant.38) | copy-start | bytes 196612
  7.7 33.5 %all-to-all-start = ((bf16[32,2,8,1024]{3,2,1,0:T(8,128)(2,1)}), bf16[32,2,8,1024]{3,2,1,0:T(8,128)(2,1)S(1)}, u32[]{:S(2)}, u32[]{:S(2)}) async-start(bf16[32,2,8,1024]{3,2,1,0:T(8,128)(2,1)} %bitcast.31), calls=%async_computation | async-start | bytes 2097152 | tf_op jit(solution)/shard_map/all_to_all | solution.py:271
  28.3 17.0 %copy-start.8 = (s32[128,128]{1,0:T(8,128)S(1)}, s32[128,128]{1,0:T(8,128)}, u32[]{:S(2)}) copy-start(s32[128,128]{1,0:T(8,128)} %param.8) | copy-start | bytes 196612
  28.3 17.1 %copy-start.11 = (s32[128]{0:T(128)S(1)}, s32[128]{0:T(128)}, u32[]{:S(2)}) copy-start(s32[128]{0:T(128)} %refs_0_.1) | copy-start | bytes 1540
  41.1 1.0 copy-start.7
  41.1 11.8 %copy-start.10 = (s32[4]{0:T(128)S(1)}, s32[4]{0:T(128)}, u32[]{:S(2)}) copy-start(s32[4]{0:T(128)} %param.10) | copy-start | bytes 52
  41.1 13.3 %copy-start.9 = (f32[2,4]{1,0:T(2,128)S(1)}, f32[2,4]{1,0:T(2,128)}, u32[]{:S(2)}) copy-start(f32[2,4]{1,0:T(2,128)} %param.11) | copy-start | bytes 100
  42.1 73.3 %all-to-all-start.1 = ((bf16[32,2,24,1024]{3,2,1,0:T(8,128)(2,1)}), bf16[32,2,24,1024]{3,2,1,0:T(8,128)(2,1)S(1)}, u32[]{:S(2)}, u32[]{:S(2)}) async-start(bf16[32,2,24,1024]{3,2,1,0:T(8,128)(2,1)} %bitcast.30), calls=%async_computation.1 | async-start | bytes 6291456 | tf_op jit(solution)/shard_map/all_to_all | solution.py:271
  146.7 31.2 %all-to-all-start.5 = ((bf16[32,2,8,1024]{3,2,1,0:T(8,128)(2,1)}), bf16[32,2,8,1024]{3,2,1,0:T(8,128)(2,1)S(1)}, u32[]{:S(2)}, u32[]{:S(2)}) async-start(bf16[32,2,8,1024]{3,2,1,0:T(8,128)(2,1)} %get-tuple-element.16), calls=%async_computation.5 | async-start | bytes 2097152 | tf_op jit(solution)/shard_map/all_to_all | solution.py:301
  151.5 3.4 %copy-start.1 = (bf16[2048,2048]{1,0:T(8,128)(2,1)S(1)}, bf16[2048,2048]{1,0:T(8,128)(2,1)}, u32[]{:S(2)}) copy-start(bf16[2048,2048]{1,0:T(8,128)(2,1)} %get-tuple-element.15.refs_1_) | copy-start | bytes 25165828
  154.9 2.2 copy-start.4
  177.9 29.5 %all-to-all-start.4 = ((bf16[32,2,8,1024]{3,2,1,0:T(8,128)(2,1)}), bf16[32,2,8,1024]{3,2,1,0:T(8,128)(2,1)S(1)}, u32[]{:S(2)}, u32[]{:S(2)}) async-start(bf16[32,2,8,1024]{3,2,1,0:T(8,128)(2,1)} %solve.5), calls=%async_computation.4 | async-start | bytes 2097152 | tf_op jit(solution)/shard_map/all_to_all | solution.py:301
  181.1 3.4 %copy-start.2 = (bf16[2048,2048]{1,0:T(8,128)(2,1)S(1)}, bf16[2048,2048]{1,0:T(8,128)(2,1)}, u32[]{:S(2)}) copy-start(bf16[2048,2048]{1,0:T(8,128)(2,1)} %get-tuple-element.15.refs_1_) | copy-start | bytes 25165828
  184.4 2.2 copy-start.5
  207.4 29.5 %all-to-all-start.3 = ((bf16[32,2,8,1024]{3,2,1,0:T(8,128)(2,1)}), bf16[32,2,8,1024]{3,2,1,0:T(8,128)(2,1)S(1)}, u32[]{:S(2)}, u32[]{:S(2)}) async-start(bf16[32,2,8,1024]{3,2,1,0:T(8,128)(2,1)} %solve.4), calls=%async_computation.3 | async-start | bytes 2097152 | tf_op jit(solution)/shard_map/all_to_all | solution.py:301
  210.6 3.4 %copy-start.3 = (bf16[2048,2048]{1,0:T(8,128)(2,1)S(1)}, bf16[2048,2048]{1,0:T(8,128)(2,1)}, u32[]{:S(2)}) copy-start(bf16[2048,2048]{1,0:T(8,128)(2,1)} %get-tuple-element.15.refs_1_) | copy-start | bytes 25165828
  214.0 2.2 copy-start.6
  216.2 24.6 %copy-start = (bf16[64,512]{1,0:T(8,128)(2,1)S(1)}, bf16[64,512]{1,0:T(8,128)(2,1)}, u32[]{:S(2)}) copy-start(bf16[64,512]{1,0:T(8,128)(2,1)} %constant.37.clone.table_ref) | copy-start | bytes 196612
  236.9 29.6 %all-to-all-start.2 = ((bf16[32,2,8,1024]{3,2,1,0:T(8,128)(2,1)}), bf16[32,2,8,1024]{3,2,1,0:T(8,128)(2,1)}, u32[]{:S(2)}, u32[]{:S(2)}) async-start(bf16[32,2,8,1024]{3,2,1,0:T(8,128)(2,1)} %solve.3), calls=%async_computation.2 | async-start | bytes 2097152 | tf_op jit(solution)/shard_map/all_to_all | solution.py:301
